TPU v7x, 32 devices: a whole 2x2x4 slice. The times are simulated.
32 devices in a mesh: section: 4 (over x, core), tensor: 8 (over z, y).
Axes of the slice: x: 2, y: 2, z: 4, core: 2. Of those that a mesh axis runs over, the one named last changes fastest.
Arguments:
- hidden: bfloat16 [256, 8192], P('section', 'tensor'), may hold values from -30 to 30
- audio: bfloat16 [128, 8192], P('section', 'tensor'), may hold values from -30 to 30
- audio_dest: int32 [128, 1], replicated, may hold values from 0 to 3; in each aligned block of 32 rows (0 to 31, 32 to 63, ...) at most 16 rows name the same one
- segment: int32 [8, 64], replicated, may hold values from 0 to 3, never falling along the last dimension, each value on 1 to 32 neighbouring positions
- norm_gain: bfloat16 [4, 8192], P('section', 'tensor'), may hold values from 0.25 to 1.75
- w_query: bfloat16 [4, 8192, 1024], P('section', None, 'tensor'), may hold values from -1 to 1
- w_keyval: bfloat16 [4, 8192, 1024], P('section', 'tensor'), may hold values from -1 to 1
- w_out: bfloat16 [4, 1024, 8192], P('section', None, 'tensor'), may hold values from -0.1875 to 0.1875
Outputs:
- lap_state: bfloat16 [512, 8192], P('section', 'tensor')
Inputs may be any that keep to these rules, and one draw needn't show every extreme that they name: `audio_dest`: in each aligned block of 32 rows (the audio rows of one stop) no stop is named more than 16 times, a bound that some block reaches.
All inputs are finite; a program needn't handle non-finite values.
Results may differ from a plain program's by a relative error of at most 0.018.
Values may be sent and summed in bfloat16 or wider, within the bound.
A program may use at most 64 MiB of HBM per device.

v0:
```python
import math

import jax
import jax.numpy as jnp
from jax import lax
from jax.sharding import PartitionSpec as P

D = 8192
HD = 128
KVH = 4
MB_DEV = 2
AUD_MB = 32
TXT_MB = 32
AUD_DEV = 32
STEPS = 4
MB_ROWS = 64


def from_behind(block, axis, distance):
    devices = range(lax.axis_size(axis))
    route = [((i - distance) % len(devices), i) for i in devices]
    return lax.ppermute(block, axis, route)


def rotate(values, cosine, sine):
    half = values.shape[-1] // 2
    first = values[..., :half]
    second = values[..., half:]
    return jnp.concatenate([first * cosine - second * sine, second * cosine + first * sine], -1)


def rope_tables(rows, width):
    position = jnp.arange(rows, dtype=jnp.float32)
    freq = 500000.0 ** (-(2.0 * jnp.arange(width // 2, dtype=jnp.float32)) / width)
    angle = position[:, None] * freq[None, :]
    return (jnp.cos(angle), jnp.sin(angle))


def local(hidden, audio, audio_dest, segment, norm_gain, w_query, w_keyval, w_out):
    stop_count = lax.axis_size("section")
    width_share = hidden.shape[1]
    section_index = lax.axis_index("section")
    part_index = lax.axis_index("tensor")
    capacity = MB_DEV * AUD_MB // stop_count
    heads = w_out.shape[1] // HD
    group_index = part_index // (heads // KVH)
    slot_count = MB_DEV * AUD_MB
    row_total = MB_DEV * MB_ROWS
    targets = audio_dest[:, 0].reshape(stop_count, AUD_DEV)
    order = jnp.arange(AUD_DEV, dtype=jnp.int32)
    earlier = order[None, :] < order[:, None]
    row_rank = jnp.sum(
        ((targets[:, :, None] == targets[:, None, :]) & earlier[None]).astype(jnp.int32), axis=2
    )
    sources = jnp.arange(stop_count, dtype=jnp.int32)[:, None]
    slot_index = sources * capacity + row_rank
    slot_ids = jnp.arange(slot_count, dtype=jnp.int32)
    every_row = lax.all_gather(audio, "section", axis=0, tiled=True)
    chosen = (slot_ids[:, None] == slot_index.reshape(-1)[None, :]) & (
        targets.reshape(-1) == section_index
    )[None, :]
    audio_slots = jnp.dot(
        chosen.astype(jnp.bfloat16), every_row, preferred_element_type=jnp.float32
    ).astype(jnp.bfloat16)
    state = jnp.concatenate(
        [
            audio_slots.reshape(MB_DEV, AUD_MB, width_share),
            hidden.reshape(MB_DEV, TXT_MB, width_share),
        ],
        1,
    )
    state = state.reshape(row_total, width_share)
    owner = slot_ids // capacity
    stop_ids = jnp.arange(stop_count, dtype=jnp.int32)
    gain_local = norm_gain[0].astype(jnp.float32)
    cosine, sine = rope_tables(MB_ROWS, HD)
    row_ids = jnp.arange(MB_ROWS, dtype=jnp.int32)
    causal = row_ids[None, :] <= row_ids[:, None]
    diagonal = row_ids[None, :] == row_ids[:, None]
    w_q = w_query[0]
    w_kv = w_keyval[0]
    w_o = w_out[0]
    scale = 1.0 / math.sqrt(HD)
    for lap_step in range(STEPS):
        root = (section_index - lap_step) % stop_count
        segment_now = lax.dynamic_slice_in_dim(segment, root * MB_DEV, MB_DEV, 0)
        counts = jnp.sum((targets == root).astype(jnp.int32), axis=1)
        per_slot = jnp.sum(
            jnp.where(owner[:, None] == stop_ids[None, :], counts[None, :], 0), axis=1
        )
        audio_live = (slot_ids % capacity < per_slot).reshape(MB_DEV, AUD_MB)
        allowed = (
            causal[None]
            & (segment_now[:, :, None] == segment_now[:, None, :])
            & (
                jnp.concatenate([audio_live, jnp.ones((MB_DEV, TXT_MB), jnp.bool_)], 1)[:, None, :]
                | diagonal[None]
            )
        )
        state_wide = state.astype(jnp.float32)
        squares = lax.psum(jnp.sum(state_wide * state_wide, axis=1), "tensor")
        inverse = lax.rsqrt(squares / D + 1e-05)[:, None]
        normed_local = (state_wide * inverse * gain_local[None, :]).astype(jnp.bfloat16)
        normed = lax.all_gather(normed_local, "tensor", axis=1, tiled=True)
        partial_kv = jnp.dot(normed_local, w_kv, preferred_element_type=jnp.float32)
        key_values = lax.psum(partial_kv, "tensor")
        own_block = lax.dynamic_slice_in_dim(key_values, group_index * 2 * HD, 2 * HD, 1)
        key_rows = rotate(own_block[:, :HD].reshape(MB_DEV, MB_ROWS, HD), cosine, sine).astype(
            jnp.bfloat16
        )
        value_rows = own_block[:, HD:].reshape(MB_DEV, MB_ROWS, HD).astype(jnp.bfloat16)
        queries = jnp.dot(normed, w_q, preferred_element_type=jnp.float32).reshape(
            MB_DEV, MB_ROWS, HD
        )
        queries = rotate(queries, cosine, sine).astype(jnp.bfloat16)
        scores = (
            jnp.einsum("mid,mjd->mij", queries, key_rows, preferred_element_type=jnp.float32)
            * scale
        )
        scores = jnp.where(allowed, scores, -jnp.inf)
        highest = jnp.max(scores, axis=-1, keepdims=True)
        weights = jnp.exp(scores - highest)
        probs = (weights / jnp.sum(weights, axis=-1, keepdims=True)).astype(jnp.bfloat16)
        attended = jnp.einsum("mij,mjd->mid", probs, value_rows, preferred_element_type=jnp.float32)
        attended = attended.astype(jnp.bfloat16).reshape(row_total, HD)
        projected = jnp.dot(
            lax.all_gather(attended, "tensor", axis=1, tiled=True),
            w_o,
            preferred_element_type=jnp.float32,
        )
        state = (state_wide + projected).astype(jnp.bfloat16)
        state = from_behind(state, "section", 1)
    return state


def solution(mesh):
    in_specs = (
        P("section", "tensor"),
        P("section", "tensor"),
        P(),
        P(),
        P("section", "tensor"),
        P("section", None, "tensor"),
        P("section", "tensor", None),
        P("section", None, "tensor"),
    )
    out_specs = P("section", "tensor")
    return jax.shard_map(local, mesh=mesh, in_specs=in_specs, out_specs=out_specs, check_vma=False)
```

profile of v0, /device:TPU:0, one launch (start us, length us, event | category | flops | bytes accessed | tf_op | source)
XLA Modules:
  0.0 745.8 jit_solution(17572982649622721375)
XLA Ops:
  7.9 1.3 reduce.4
  10.3 7.4 all_gather.27
  19.1 21.7 %psum.56 = f32[128]{0:T(128)S(1)} all-reduce(f32[128]{0:T(128)S(1)} %reduce_sum.168), channel_id=1, replica_groups=mesh['section'=4,'tensor'=8] {'tensor'}, use_global_device_ids=true, to_apply=%region_4.5 | all-reduce | flops 128 | bytes 1024 | tf_op jit(solution)/shard_map/psum | solution.py:101
  45.0 68.0 %all-reduce.9.cloned.1.call-done = f32[128,1024]{1,0:T(8,128)} async-done(((f32[128,1024]{1,0:T(8,128)}), f32[128,1024]{1,0:T(8,128)}) %all-reduce.9.cloned.1.call-update) | async-done | bytes 524304 | tf_op jit(solution)/shard_map/psum | solution.py:106
  114.8 49.3 %all-gather.5.cloned.1.call-done = bf16[128,8192]{1,0:T(8,128)(2,1)} async-done(((bf16[128,1024]{1,0:T(8,128)(2,1)}), bf16[128,8192]{1,0:T(8,128)(2,1)}) %all-gather.5.cloned.1.call-update) | async-done | bytes 2097168 | tf_op jit(solution)/shard_map/all_gather | solution.py:104
  164.1 2.9 fusion.26
  167.8 26.5 %all_gather.29 = bf16[128,1024]{1,0:T(8,128)(2,1)S(1)} all-gather(bf16[128,128]{1,0:T(8,128)(2,1)S(1)} %bitcast.117), channel_id=1, replica_groups=mesh['section'=4,'tensor'=8] {'tensor'}, dimensions={1}, use_global_device_ids=true | all-gather | bytes 294912 | tf_op jit(solution)/shard_map/all_gather | solution.py:127
  194.3 2.0 fusion.49
  196.4 5.8 collective-permute-done
  202.3 17.6 %psum.58 = f32[128]{0:T(128)S(1)} all-reduce(f32[128]{0:T(128)S(1)} %fusion.64), channel_id=1, replica_groups=mesh['section'=4,'tensor'=8] {'tensor'}, use_global_device_ids=true, to_apply=%region_11.12 | all-reduce | flops 128 | bytes 1024 | tf_op jit(solution)/shard_map/psum | solution.py:101
  222.0 70.0 %all-reduce.11.cloned.1.call-done = f32[128,1024]{1,0:T(8,128)} async-done(((f32[128,1024]{1,0:T(8,128)}), f32[128,1024]{1,0:T(8,128)}) %all-reduce.11.cloned.1.call-update) | async-done | bytes 524304 | tf_op jit(solution)/shard_map/psum | solution.py:106
  293.7 48.9 %all-gather.7.cloned.1.call-done = bf16[128,8192]{1,0:T(8,128)(2,1)} async-done(((bf16[128,1024]{1,0:T(8,128)(2,1)}), bf16[128,8192]{1,0:T(8,128)(2,1)}) %all-gather.7.cloned.1.call-update) | async-done | bytes 2097168 | tf_op jit(solution)/shard_map/all_gather | solution.py:104
  342.7 2.9 fusion.24
  346.4 26.5 %all_gather.31 = bf16[128,1024]{1,0:T(8,128)(2,1)S(1)} all-gather(bf16[128,128]{1,0:T(8,128)(2,1)S(1)} %bitcast.118), channel_id=1, replica_groups=mesh['section'=4,'tensor'=8] {'tensor'}, dimensions={1}, use_global_device_ids=true | all-gather | bytes 294912 | tf_op jit(solution)/shard_map/all_gather | solution.py:127
  372.8 2.0 fusion.46
  374.9 5.8 collective-permute-done.1
  380.9 17.6 %psum.60 = f32[128]{0:T(128)S(1)} all-reduce(f32[128]{0:T(128)S(1)} %fusion.67), channel_id=1, replica_groups=mesh['section'=4,'tensor'=8] {'tensor'}, use_global_device_ids=true, to_apply=%region_18.19 | all-reduce | flops 128 | bytes 1024 | tf_op jit(solution)/shard_map/psum | solution.py:101
  398.7 1.3 fusion.14
  400.8 69.9 %all-reduce.13.cloned.1.call-done = f32[128,1024]{1,0:T(8,128)} async-done(((f32[128,1024]{1,0:T(8,128)}), f32[128,1024]{1,0:T(8,128)}) %all-reduce.13.cloned.1.call-update) | async-done | bytes 524304 | tf_op jit(solution)/shard_map/psum | solution.py:106
  472.3 49.2 %all-gather.9.cloned.1.call-done = bf16[128,8192]{1,0:T(8,128)(2,1)} async-done(((bf16[128,1024]{1,0:T(8,128)(2,1)}), bf16[128,8192]{1,0:T(8,128)(2,1)}) %all-gather.9.cloned.1.call-update) | async-done | bytes 2097168 | tf_op jit(solution)/shard_map/all_gather | solution.py:104
  521.5 2.9 fusion.22
  525.2 26.5 %all_gather.33 = bf16[128,1024]{1,0:T(8,128)(2,1)S(1)} all-gather(bf16[128,128]{1,0:T(8,128)(2,1)S(1)} %bitcast.119), channel_id=1, replica_groups=mesh['section'=4,'tensor'=8] {'tensor'}, dimensions={1}, use_global_device_ids=true | all-gather | bytes 294912 | tf_op jit(solution)/shard_map/all_gather | solution.py:127
  551.7 2.0 fusion.43
  553.8 5.8 collective-permute-done.2
  559.7 17.6 %psum.62 = f32[128]{0:T(128)S(1)} all-reduce(f32[128]{0:T(128)S(1)} %fusion.70), channel_id=1, replica_groups=mesh['section'=4,'tensor'=8] {'tensor'}, use_global_device_ids=true, to_apply=%region_25.26 | all-reduce | flops 128 | bytes 1024 | tf_op jit(solution)/shard_map/psum | solution.py:101
  577.5 1.3 fusion.12
  579.6 69.9 %all-reduce.15.cloned.1.call-done = f32[128,1024]{1,0:T(8,128)} async-done(((f32[128,1024]{1,0:T(8,128)}), f32[128,1024]{1,0:T(8,128)}) %all-reduce.15.cloned.1.call-update) | async-done | bytes 524304 | tf_op jit(solution)/shard_map/psum | solution.py:106
  651.1 49.1 %all-gather.11.cloned.1.call-done = bf16[128,8192]{1,0:T(8,128)(2,1)} async-done(((bf16[128,1024]{1,0:T(8,128)(2,1)}), bf16[128,8192]{1,0:T(8,128)(2,1)}) %all-gather.11.cloned.1.call-update) | async-done | bytes 2097168 | tf_op jit(solution)/shard_map/all_gather | solution.py:104
  700.2 2.9 fusion.20
  704.0 26.5 %all_gather.35 = bf16[128,1024]{1,0:T(8,128)(2,1)S(1)} all-gather(bf16[128,128]{1,0:T(8,128)(2,1)S(1)} %bitcast.120), channel_id=1, replica_groups=mesh['section'=4,'tensor'=8] {'tensor'}, dimensions={1}, use_global_device_ids=true | all-gather | bytes 294912 | tf_op jit(solution)/shard_map/all_gather | solution.py:127
  730.4 2.0 fusion.40
  732.5 5.8 collective-permute-done.3
  (102 shorter events, 23.0 us)
Async XLA Ops:
  6.5 35.4 %copy-start = (bf16[1,1024,1024]{2,1,0:T(8,128)(2,1)S(1)}, bf16[1,1024,1024]{2,1,0:T(8,128)(2,1)}, u32[]{:S(2)}) copy-start(bf16[1,1024,1024]{2,1,0:T(8,128)(2,1)} %param.14) | copy-start | bytes 6291460
  6.5 106.6 %all-reduce.9.cloned.1.call-start = ((), (), s32[]{:S(2)}) async-start(), calls=%async_computation.1 | async-start | bytes 1048576 | tf_op jit(solution)/shard_map/psum | solution.py:106
  17.9 25.4 %copy-start.4 = (bf16[64,1024]{1,0:T(8,128)(2,1)S(1)}, bf16[64,1024]{1,0:T(8,128)(2,1)}, u32[]{:S(2)}) copy-start(bf16[64,1024]{1,0:T(8,128)(2,1)} %param.8) | copy-start | bytes 393220
  42.0 2.8 copy-start.5
  43.3 120.8 %all-gather.5.cloned.1.call-start = ((), (), s32[]{:S(2)}) async-start(), calls=%async_computation | async-start | bytes 2359296 | tf_op jit(solution)/shard_map/all_gather | solution.py:104
  44.2 247.8 %all-reduce.11.cloned.1.call-start = ((), (), s32[]{:S(2)}) async-start(), calls=%async_computation.3 | async-start | bytes 1048576 | tf_op jit(solution)/shard_map/psum | solution.py:106
  196.3 5.8 collective-permute-start
  220.1 1.3 copy-start.3
  221.4 121.3 %all-gather.7.cloned.1.call-start = ((), (), s32[]{:S(2)}) async-start(), calls=%async_computation.2 | async-start | bytes 2359296 | tf_op jit(solution)/shard_map/all_gather | solution.py:104
  222.0 248.7 %all-reduce.13.cloned.1.call-start = ((), (), s32[]{:S(2)}) async-start(), calls=%async_computation.5 | async-start | bytes 1048576 | tf_op jit(solution)/shard_map/psum | solution.py:106
  374.9 5.8 collective-permute-start.1
  398.7 1.3 copy-start.1
  400.0 121.6 %all-gather.9.cloned.1.call-start = ((), (), s32[]{:S(2)}) async-start(), calls=%async_computation.4 | async-start | bytes 2359296 | tf_op jit(solution)/shard_map/all_gather | solution.py:104
  400.5 248.9 %all-reduce.15.cloned.1.call-start = ((), (), s32[]{:S(2)}) async-start(), calls=%async_computation.7 | async-start | bytes 1048576 | tf_op jit(solution)/shard_map/psum | solution.py:106
  553.7 5.8 collective-permute-start.2
  577.5 1.3 copy-start.2
  578.8 121.4 %all-gather.11.cloned.1.call-start = ((), (), s32[]{:S(2)}) async-start(), calls=%async_computation.6 | async-start | bytes 2359296 | tf_op jit(solution)/shard_map/all_gather | solution.py:104
  732.5 5.8 collective-permute-start.3
Sparse Core Ops, SparseCore 0:
  43.4 69.6 all-reduce.8
  115.5 48.5 all-gather.4
  221.5 70.4 all-reduce.10
  294.1 48.5 all-gather.6
  400.1 70.5 all-reduce.12
  472.9 48.5 all-gather.8
  578.9 70.4 all-reduce.14
  651.6 48.5 all-gather.10
where the time goes:
time: 747 us; the launch traced here: 746 us
  waiting for transfers between devices  499 us (67%)
  blocking collectives  188 us (25%)
  matrix products  27.8 us (4%)
  between operations  14 us (2%)
  local copies, waits for them, and re-layouts  8.71 us (1%)
  other arithmetic  7.84 us (1%)
    psum x4, waiting for transfers between devices, local(): key_values = lax.psum(partial_kv, 'tensor')  278 us
    all_gather x4, waiting for transfers between devices, local(): normed = lax.all_gather(normed_local, 'tensor', axis=1, tiled=True)  196 us
    all_gather x4, blocking collectives, local(): lax.all_gather(attended, 'tensor', axis=1, tiled=True)  106 us
    psum x4, blocking collectives, local(): squares = lax.psum(jnp.sum(state_wide * state_wide, axis=1), 'tensor')  74.6 us
    ppermute x4, waiting for transfers between devices, from_behind(): return lax.ppermute(block, axis, route)  23.1 us
  transfers between devices with their start and end apart: 12, of which 12 were waited for; matrix products, arithmetic and copies ran while one was open for 1% of the time, Pallas kernels for 0%

commit v1 on v0

v1 whole, which is shorter than its diff:
```python
import functools
import math

import jax
import jax.numpy as jnp
import numpy as np
from jax import lax
from jax.experimental import pallas as pl
from jax.experimental.pallas import tpu as pltpu
from jax.sharding import PartitionSpec as P

D = 8192
HD = 128
KVH = 4
MB_DEV = 2
AUD_MB = 32
TXT_MB = 32
AUD_DEV = 32
STEPS = 4
MB_ROWS = 64
MESH = pl.DeviceIdType.MESH
F32 = jnp.float32
BF16 = jnp.bfloat16


def rope_tables():
    position = np.arange(MB_ROWS, dtype=np.float32)
    freq = np.float32(500000.0) ** (-(2.0 * np.arange(HD // 2, dtype=np.float32)) / HD)
    angle = (position[:, None] * freq[None, :].astype(np.float32)).astype(np.float32)
    cosine, sine = np.cos(angle), np.sin(angle)
    return (
        np.concatenate([cosine, cosine], 1).astype(np.float32),
        np.concatenate([-sine, sine], 1).astype(np.float32),
    )


def iota(shape, dim):
    return lax.broadcasted_iota(jnp.int32, shape, dim)


def drain(ref, sem):
    pltpu.make_async_copy(ref, ref, sem).wait()


def kernel(
    S,
    T,
    hidden,
    audio,
    dest,
    segment,
    gain,
    wq,
    wkv,
    wo_hbm,
    cos_ref,
    sin_ref,
    out,
    w_all,
    wo,
    arecv,
    hid,
    xs,
    xnew,
    psend,
    yrecv,
    accum,
    zsend,
    zrecv,
    sssend,
    ssrecv,
    kvsend,
    kvrecv,
    att,
    local_sem,
    w_sems,
    a_sems,
    send_sems,
    recv_sems,
):
    Z = T // 2
    width = gain.shape[1]
    cap = MB_DEV * AUD_MB // S
    shift = cap.bit_length() - 1
    per_kv = Z // KVH
    q_cols = Z * HD
    me = lax.axis_index("section")
    t = lax.axis_index("tensor")
    y = lax.rem(t, 2)
    z = lax.div(t, 2)
    partner = t + 1 - 2 * y

    def lanes(index):
        return pl.ds(pl.multiple_of(index * HD, HD), HD)

    def tensor_peer(k):
        return lax.rem(t + k, T)

    def push(src, dst, send, recv, device):
        pltpu.make_async_remote_copy(
            src_ref=src,
            dst_ref=dst,
            send_sem=send,
            recv_sem=recv,
            device_id=device,
            device_id_type=MESH,
        ).start()

    stage = [
        pltpu.make_async_copy(
            wq.at[0, pl.ds(pl.multiple_of(t * width, width), width), :],
            w_all.at[y, :, lanes(z)],
            local_sem.at[0],
        ),
        pltpu.make_async_copy(audio, arecv.at[me], local_sem.at[1]),
        pltpu.make_async_copy(hidden, hid, local_sem.at[2]),
        pltpu.make_async_copy(wo_hbm.at[0], wo, local_sem.at[3]),
    ]
    for h in range(KVH):
        for part in range(2):
            stage.append(
                pltpu.make_async_copy(
                    wkv.at[0, :, pl.ds((2 * h + part) * HD, HD)],
                    w_all.at[part, :, pl.ds(q_cols + h * HD, HD)],
                    local_sem.at[4 + 2 * h + part],
                )
            )

    barrier = pltpu.get_barrier_semaphore()
    for k in range(1, T):
        pl.semaphore_signal(
            barrier, inc=1, device_id={"tensor": tensor_peer(k)}, device_id_type=MESH
        )
    for k in range(1, S):
        pl.semaphore_signal(
            barrier, inc=1, device_id={"section": lax.rem(me + k, S)}, device_id_type=MESH
        )
    for copy in stage:
        copy.start()
    pl.semaphore_wait(barrier, T + S - 2)

    for k in range(1, S):
        push(
            audio,
            arecv.at[me],
            a_sems.at[0],
            a_sems.at[1],
            {"section": lax.rem(me + k, S)},
        )
    for k in range(1, T):
        peer = tensor_peer(k)
        push(
            wq.at[0, pl.ds(pl.multiple_of(peer * width, width), width), :],
            w_all.at[y, :, lanes(z)],
            w_sems.at[0],
            w_sems.at[1],
            {"tensor": peer},
        )

    N = dest.shape[0]
    dcol = dest[...].astype(F32)
    sub, lane = iota((N, N), 0), iota((N, N), 1)
    drow = jnp.sum(jnp.where(sub == lane, dcol, 0.0), axis=0, keepdims=True)
    same = (dcol == drow) & ((sub >> 5) == (lane >> 5)) & (sub < lane)
    rank = jnp.sum(jnp.where(same, 1.0, 0.0), axis=0, keepdims=True)
    block = (iota((1, N), 1) >> 5).astype(F32)
    slot = block * float(cap) + rank
    mine = drow == me.astype(F32)

    for copy in stage:
        copy.wait()
    drain(arecv.at[pl.ds(0, S - 1)], a_sems.at[1])
    every_row = arecv[...].reshape(N, width)
    for m in range(MB_DEV):
        wanted = (iota((AUD_MB, N), 0) + m * AUD_MB).astype(F32)
        chosen = jnp.where((slot == wanted) & mine, 1.0, 0.0).astype(BF16)
        rows = jnp.dot(chosen, every_row, preferred_element_type=F32)
        xs[0, m, 0:AUD_MB, :] = rows.astype(BF16)
        xs[0, m, AUD_MB:MB_ROWS, :] = hid[m * TXT_MB : (m + 1) * TXT_MB, :]

    eye = iota((MB_ROWS, MB_ROWS), 0) == iota((MB_ROWS, MB_ROWS), 1)
    causal = iota((MB_ROWS, MB_ROWS), 1) <= iota((MB_ROWS, MB_ROWS), 0)
    scale = 1.0 / math.sqrt(HD)

    def to_col(row):
        return jnp.sum(jnp.where(eye, row, 0.0), axis=1, keepdims=True)

    def to_row(col):
        return jnp.sum(jnp.where(eye, col, 0.0), axis=0, keepdims=True)

    def allowed_of(root, m):
        seg_row = segment[pl.ds(root * MB_DEV + m, 1), :].astype(F32)
        seg_col = to_col(seg_row)
        position = iota((MB_ROWS, N), 0)
        owner = ((position + m * AUD_MB) >> shift).astype(F32)
        named = (drow == root.astype(F32)) & (block == owner)
        count = jnp.sum(jnp.where(named, 1.0, 0.0), axis=1, keepdims=True)
        index = iota((MB_ROWS, 1), 0)
        within = (index & (cap - 1)).astype(F32)
        live = jnp.where((within < count) | (index >= AUD_MB), 1.0, 0.0)
        return causal & (seg_col == seg_row) & ((to_row(live) > 0.5) | eye)

    def body(s, carry):
        root = lax.rem(me - s + 2 * S, S)
        masks = []
        for m in range(MB_DEV):

            @pl.when(s > 0)
            def _():
                drain(xs.at[s, m], recv_sems.at[s, m, 5])

            x = xs[s, m].astype(F32)
            square = x * x
            high = square.astype(BF16)
            low = (square - high.astype(F32)).astype(BF16)
            ones = jnp.ones((8, width), BF16)
            contract = (((1,), (1,)), ((), ()))
            sums = lax.dot_general(ones, high, contract, preferred_element_type=F32)
            sums = sums + lax.dot_general(ones, low, contract, preferred_element_type=F32)
            sssend[s, m] = jnp.concatenate([sums, sums], axis=1)
            for k in range(1, T):
                push(
                    sssend.at[s, m],
                    ssrecv.at[s, m, k - 1],
                    send_sems.at[s, m, 0],
                    recv_sems.at[s, m, 0],
                    {"tensor": tensor_peer(k)},
                )
            xg = (x * gain[...].astype(F32)).astype(BF16)
            if m == 0:

                @pl.when(s == 0)
                def _():
                    drain(wq.at[0, pl.ds(0, (T - 1) * width), :], w_sems.at[1])

            theirs = jnp.dot(xg, w_all[1 - y], preferred_element_type=F32)
            psend[s, m] = theirs.astype(BF16)
            push(
                psend.at[s, m],
                yrecv.at[s, m],
                send_sems.at[s, m, 1],
                recv_sems.at[s, m, 1],
                {"tensor": partner},
            )
            accum[m] = jnp.dot(xg, w_all[y], preferred_element_type=F32)

        for m in range(MB_DEV):
            masks.append(allowed_of(root, m))

        for m in range(MB_DEV):
            drain(yrecv.at[s, m], recv_sems.at[s, m, 1])
            accum[m] = accum[m] + yrecv[s, m].astype(F32)
            for k in range(1, Z):
                other = lax.rem(z + k, Z)
                head = lax.div(other, per_kv)
                zsend[s, m, k - 1, :, 0:HD] = accum[m, :, lanes(other)].astype(BF16)
                zsend[s, m, k - 1, :, HD : 2 * HD] = accum[m, :, lanes(Z + head)].astype(BF16)
                push(
                    zsend.at[s, m, k - 1],
                    zrecv.at[s, m, k - 1],
                    send_sems.at[s, m, 2],
                    recv_sems.at[s, m, 2],
                    {"tensor": other * 2 + y},
                )

        cosine, sine = cos_ref[...], sin_ref[...]
        is_key = y == 0
        cos_kv = jnp.where(is_key, cosine, 1.0)
        sin_kv = jnp.where(is_key, sine, 0.0)
        queries = []
        for m in range(MB_DEV):
            drain(ssrecv.at[s, m], recv_sems.at[s, m, 0])
            total = sssend[s, m] + jnp.sum(ssrecv[s, m], axis=0)
            inverse = lax.rsqrt(total[0:1, 0:MB_ROWS] / D + 1e-05)
            inverse = to_col(inverse)
            drain(zrecv.at[s, m], recv_sems.at[s, m, 2])
            head = lax.div(z, per_kv)
            arrived = jnp.sum(zrecv[s, m].astype(F32), axis=0)
            keyval = (accum[m, :, lanes(Z + head)] + arrived[:, HD:]) * inverse
            keyval = keyval * cos_kv + pltpu.roll(keyval, HD // 2, 1) * sin_kv
            kvsend[s, m] = keyval.astype(BF16)
            push(
                kvsend.at[s, m],
                kvrecv.at[s, m],
                send_sems.at[s, m, 3],
                recv_sems.at[s, m, 3],
                {"tensor": partner},
            )
            query = (accum[m, :, lanes(z)] + arrived[:, :HD]) * inverse
            query = query * cosine + pltpu.roll(query, HD // 2, 1) * sine
            queries.append(query.astype(BF16))

        for m in range(MB_DEV):
            drain(kvrecv.at[s, m], recv_sems.at[s, m, 3])
            own, got = kvsend[s, m], kvrecv[s, m]
            keys = jnp.where(is_key, own, got)
            values = jnp.where(is_key, got, own)
            scores = lax.dot_general(
                queries[m], keys, (((1,), (1,)), ((), ())), preferred_element_type=F32
            )
            scores = jnp.where(masks[m], scores * scale, -jnp.inf)
            highest = jnp.max(scores, axis=-1, keepdims=True)
            weights = jnp.exp(scores - highest)
            probs = (weights / jnp.sum(weights, axis=-1, keepdims=True)).astype(BF16)
            attended = jnp.dot(probs, values, preferred_element_type=F32)
            att[s, m, :, lanes(t)] = attended.astype(BF16)
            for k in range(1, T):
                push(
                    att.at[s, m, :, lanes(t)],
                    att.at[s, m, :, lanes(t)],
                    send_sems.at[s, m, 4],
                    recv_sems.at[s, m, 4],
                    {"tensor": tensor_peer(k)},
                )

        for m in range(MB_DEV):
            drain(att.at[s, m, :, pl.ds(0, (T - 1) * HD)], recv_sems.at[s, m, 4])
            projected = jnp.dot(att[s, m], wo[...], preferred_element_type=F32)
            xnew[s, m] = (xs[s, m].astype(F32) + projected).astype(BF16)
            push(
                xnew.at[s, m],
                xs.at[s + 1, m],
                send_sems.at[s, m, 5],
                recv_sems.at[s + 1, m, 5],
                {"section": lax.rem(me + 1, S)},
            )
        return carry

    lax.fori_loop(0, STEPS, body, 0)

    for m in range(MB_DEV):
        drain(xs.at[STEPS, m], recv_sems.at[STEPS, m, 5])
        out[m * MB_ROWS : (m + 1) * MB_ROWS, :] = xs[STEPS, m]

    drain(arecv.at[pl.ds(0, S - 1)], a_sems.at[0])
    drain(wq.at[0, pl.ds(0, (T - 1) * width), :], w_sems.at[0])

    def finish(s, carry):
        for m in range(MB_DEV):
            drain(ssrecv.at[s, m], send_sems.at[s, m, 0])
            drain(psend.at[s, m], send_sems.at[s, m, 1])
            drain(zsend.at[s, m], send_sems.at[s, m, 2])
            drain(kvsend.at[s, m], send_sems.at[s, m, 3])
            drain(att.at[s, m, :, pl.ds(0, (T - 1) * HD)], send_sems.at[s, m, 4])
            drain(xnew.at[s, m], send_sems.at[s, m, 5])
        return carry

    lax.fori_loop(0, STEPS, finish, 0)


def local(S, T, hidden, audio, audio_dest, segment, norm_gain, w_query, w_keyval, w_out):
    width = hidden.shape[1]
    rows = MB_DEV * MB_ROWS
    Z = T // 2
    cols = (Z + KVH) * HD
    cosine, sine = rope_tables()
    vmem = pl.BlockSpec(memory_space=pltpu.VMEM)
    hbm = pl.BlockSpec(memory_space=pl.ANY)
    per = (STEPS, MB_DEV)
    scratch = [
        pltpu.VMEM((2, width, cols), BF16),
        pltpu.VMEM(w_out.shape[1:], BF16),
        pltpu.VMEM((S, AUD_DEV, width), BF16),
        pltpu.VMEM((MB_DEV * TXT_MB, width), BF16),
        pltpu.VMEM((STEPS + 1, MB_DEV, MB_ROWS, width), BF16),
        pltpu.VMEM(per + (MB_ROWS, width), BF16),
        pltpu.VMEM(per + (MB_ROWS, cols), BF16),
        pltpu.VMEM(per + (MB_ROWS, cols), BF16),
        pltpu.VMEM((MB_DEV, MB_ROWS, cols), F32),
        pltpu.VMEM(per + (Z - 1, MB_ROWS, 2 * HD), BF16),
        pltpu.VMEM(per + (Z - 1, MB_ROWS, 2 * HD), BF16),
        pltpu.VMEM(per + (8, 2 * MB_ROWS), F32),
        pltpu.VMEM(per + (T - 1, 8, 2 * MB_ROWS), F32),
        pltpu.VMEM(per + (MB_ROWS, HD), BF16),
        pltpu.VMEM(per + (MB_ROWS, HD), BF16),
        pltpu.VMEM(per + (MB_ROWS, T * HD), BF16),
        pltpu.SemaphoreType.DMA((4 + 2 * KVH,)),
        pltpu.SemaphoreType.DMA((2,)),
        pltpu.SemaphoreType.DMA((2,)),
        pltpu.SemaphoreType.DMA(per + (6,)),
        pltpu.SemaphoreType.DMA((STEPS + 1, MB_DEV, 6)),
    ]
    return pl.pallas_call(
        functools.partial(kernel, S, T),
        out_shape=jax.ShapeDtypeStruct((rows, width), BF16),
        in_specs=[hbm, hbm, vmem, vmem, vmem, hbm, hbm, hbm, vmem, vmem],
        out_specs=vmem,
        scratch_shapes=scratch,
        compiler_params=pltpu.CompilerParams(
            collective_id=0, has_side_effects=True, vmem_limit_bytes=48 * 1024 * 1024
        ),
        cost_estimate=pl.CostEstimate(
            flops=STEPS * rows * width * (2 * cols + T * HD) * 2,
            bytes_accessed=8 * 1024 * 1024,
            transcendentals=0,
        ),
    )(
        hidden,
        audio,
        audio_dest,
        segment,
        norm_gain,
        w_query,
        w_keyval,
        w_out,
        jnp.asarray(cosine),
        jnp.asarray(sine),
    )


def solution(mesh):
    in_specs = (
        P("section", "tensor"),
        P("section", "tensor"),
        P(),
        P(),
        P("section", "tensor"),
        P("section", None, "tensor"),
        P("section", "tensor", None),
        P("section", None, "tensor"),
    )
    out_specs = P("section", "tensor")
    body = functools.partial(local, mesh.shape["section"], mesh.shape["tensor"])
    return jax.shard_map(body, mesh=mesh, in_specs=in_specs, out_specs=out_specs, check_vma=False)
```

time: 747 us -> 154 us (0.21)
  waiting for transfers between devices: 499 us -> 0 us
  blocking collectives: 188 us -> 0 us
  Pallas kernels: 0 us -> 144 us
  matrix products: 27.8 us -> 0 us
  between operations: 14 us -> 0.02 us
  other arithmetic: 7.84 us -> 0 us
    psum x4 -> x0, waiting for transfers between devices: 278 us -> none  [local(): key_values = lax.psum(partial_kv, 'tensor')]
    all_gather x4 -> x0, waiting for transfers between devices: 196 us -> none  [local(): normed = lax.all_gather(normed_local, 'tensor', axis=1, tiled=True)]
    pallas_call x0 -> x1, Pallas kernels: none -> 144 us  [local(): pl.pallas_call(functools.partial(kernel, S, T), out_shape=jax.ShapeDtypeS...]
    all_gather x5 -> x0, blocking collectives: 113 us -> none  [the longest x4 106 us: local(): lax.all_gather(attended, 'tensor', axis=1, tiled=True)]
    psum x4 -> x0, blocking collectives: 74.6 us -> none  [local(): squares = lax.psum(jnp.sum(state_wide * state_wide, axis=1), 'tensor')]
    dot_general x21 -> x0, matrix products: 26.7 us -> none  [the longest x4 11.7 us: local(): jnp.dot(normed, w_q, preferred_element_type=jnp.float32)]
    ppermute x4 -> x0, waiting for transfers between devices: 23.1 us -> none  [from_behind(): return lax.ppermute(block, axis, route)]
    unnamed x14 -> x18, local copies, waits for them, and re-layouts: 1.25 us -> 9.27 us
  transfers between devices with their start and end apart: 12 -> 0, of which waited for: 12 -> 0; matrix products, arithmetic and copies ran while one was open for 1% -> 0% of each run, Pallas kernels for 0% -> 0%
where the time goes in v1:
time: 154 us; the launch traced here: 153 us
  Pallas kernels  144 us (94%)
  local copies, waits for them, and re-layouts  9.27 us (6%)
    pallas_call x1, Pallas kernels, local(): pl.pallas_call(functools.partial(kernel, S, T), out_shape=jax.ShapeDtypeS...  144 us
    unnamed x18, local copies, waits for them, and re-layouts  9.27 us

profile of v1, /device:TPU:0, one launch (start us, length us, event | category | flops | bytes accessed | tf_op | source)
XLA Modules:
  0.0 153.1 jit_solution(18329431526463195214)
XLA Ops:
  0.0 0.8 copy.11.dest
  0.8 0.0 copy-start
  0.8 1.6 %copy-done = bf16[1,8192,128]{2,1,0:T(8,128)(2,1)S(1)} copy-done((bf16[1,8192,128]{2,1,0:T(8,128)(2,1)S(1)}, bf16[1,8192,128]{2,1,0:T(8,128)(2,1)}, u32[]{:S(2)}) %copy-start) | copy-done | bytes 2097176
  2.4 0.0 copy-start.1
  2.4 1.6 %copy-done.1 = bf16[1,1024,1024]{2,1,0:T(8,128)(2,1)S(1)} copy-done((bf16[1,1024,1024]{2,1,0:T(8,128)(2,1)S(1)}, bf16[1,1024,1024]{2,1,0:T(8,128)(2,1)}, u32[]{:S(2)}) %copy-start.1) | copy-done | bytes 2097176
  3.9 0.0 copy-start.2
  3.9 0.9 copy-done.2
  4.8 0.0 copy-start.3
  4.9 0.8 copy-done.3
  5.7 0.0 copy-start.4
  5.7 0.7 copy-done.4
  6.4 0.0 copy-start.5
  6.4 0.7 copy-done.5
  7.1 0.0 copy-start.6
  7.1 0.8 copy-done.6
  7.8 0.0 copy-start.7
  7.8 0.8 copy-done.7
  8.6 143.8 %shard_map.100 = bf16[128,1024]{1,0:T(8,128)(2,1)S(1)} custom-call(bf16[64,1024]{1,0:T(8,128)(2,1)S(1)} %copy-done.2, bf16[32,1024]{1,0:T(8,128)(2,1)S(1)} %copy-done.3, s32[128,1]{1,0:T(8,128)S(1)} %copy.11.dest, s32[8,64]{1,0:T(8,128)S(1)} %copy-done.4, bf16[1,1024]{1,0:T(2,128)(2,1)S(1)} %copy-done.5, bf16[1,8192,128]{2,1,0:T(8,128)(2,1)S(1)} %copy-done, ...), custom_call_target="tpu_custom_call" | custom-call | flops 3221225472 | bytes 8388608 | tf_op jit(solution)/shard_map/pallas_call | solution.py:383
  152.4 0.7 copy.13
Async XLA Ops:
  0.8 1.6 %copy-start = (bf16[1,8192,128]{2,1,0:T(8,128)(2,1)S(1)}, bf16[1,8192,128]{2,1,0:T(8,128)(2,1)}, u32[]{:S(2)}) copy-start(bf16[1,8192,128]{2,1,0:T(8,128)(2,1)} %wq.1) | copy-start | bytes 6291460
  2.4 1.6 %copy-start.1 = (bf16[1,1024,1024]{2,1,0:T(8,128)(2,1)S(1)}, bf16[1,1024,1024]{2,1,0:T(8,128)(2,1)}, u32[]{:S(2)}) copy-start(bf16[1,1024,1024]{2,1,0:T(8,128)(2,1)} %wkv.1) | copy-start | bytes 6291460
  3.9 0.9 copy-start.2
  4.8 0.8 copy-start.3
  5.7 0.7 copy-start.4
  6.4 0.7 copy-start.5
  7.1 0.8 copy-start.6
  7.8 0.8 copy-start.7

commit v2 on v1

v2 whole, which is shorter than its diff:
```python
import functools
import math

import jax
import jax.numpy as jnp
import numpy as np
from jax import lax
from jax.experimental import pallas as pl
from jax.experimental.pallas import tpu as pltpu
from jax.sharding import PartitionSpec as P

D = 8192
HD = 128
KVH = 4
MB_DEV = 2
AUD_MB = 32
TXT_MB = 32
AUD_DEV = 32
STEPS = 4
MB_ROWS = 64
MESH = pl.DeviceIdType.MESH
F32 = jnp.float32
BF16 = jnp.bfloat16


def rope_tables():
    position = np.arange(MB_ROWS, dtype=np.float32)
    freq = np.float32(500000.0) ** (-(2.0 * np.arange(HD // 2, dtype=np.float32)) / HD)
    angle = (position[:, None] * freq[None, :].astype(np.float32)).astype(np.float32)
    cosine, sine = np.cos(angle), np.sin(angle)
    return (
        np.concatenate([cosine, cosine], 1).astype(np.float32),
        np.concatenate([-sine, sine], 1).astype(np.float32),
    )


def iota(shape, dim):
    return lax.broadcasted_iota(jnp.int32, shape, dim)


def drain(ref, sem):
    pltpu.make_async_copy(ref, ref, sem).wait()


def kernel(
    S,
    T,
    hidden,
    audio,
    dest,
    segment,
    gain,
    wq,
    wkv,
    wo_hbm,
    cos_ref,
    sin_ref,
    out,
    w_all,
    wo,
    arecv,
    hid,
    gain_own,
    gain_pair,
    xs,
    xnew,
    accum,
    qsend,
    qrecv,
    kvsend,
    kvrecv,
    sssend,
    ssrecv,
    swsend,
    swrecv,
    att,
    local_sem,
    w_sems,
    send_sems,
    recv_sems,
):
    Z = T // 2
    width = gain.shape[1]
    cap = MB_DEV * AUD_MB // S
    shift = cap.bit_length() - 1
    per_kv = Z // KVH
    q_cols = Z * HD
    kv_cols = KVH * HD
    me = lax.axis_index("section")
    t = lax.axis_index("tensor")
    y = lax.rem(t, 2)
    z = lax.div(t, 2)
    partner = t + 1 - 2 * y
    after = lax.rem(me + 1, S)
    before = lax.rem(me + S - 1, S)
    own_half = pl.ds(pl.multiple_of(y * width, width), width)

    def lanes(index):
        return pl.ds(pl.multiple_of(index * HD, HD), HD)

    def pair_rows(index):
        return pl.ds(pl.multiple_of(index * 2 * width, 2 * width), 2 * width)

    def tensor_peer(k):
        return lax.rem(t + k, T)

    def line_peer(k):
        return lax.rem(z + k, Z)

    def push(src, dst, send, recv, device):
        pltpu.make_async_remote_copy(
            src_ref=src,
            dst_ref=dst,
            send_sem=send,
            recv_sem=recv,
            device_id=device,
            device_id_type=MESH,
        ).start()

    stage = [
        pltpu.make_async_copy(audio, arecv.at[me], local_sem.at[0]),
        pltpu.make_async_copy(hidden, hid, local_sem.at[1]),
    ]
    late = [
        pltpu.make_async_copy(wo_hbm.at[0], wo, local_sem.at[2]),
        pltpu.make_async_copy(
            wq.at[0, pair_rows(z), :], w_all.at[:, lanes(z)], local_sem.at[3]
        ),
    ]
    for h in range(KVH):
        late.append(
            pltpu.make_async_copy(
                wkv.at[0, :, lanes(2 * h + y)],
                w_all.at[own_half, pl.ds(q_cols + h * HD, HD)],
                local_sem.at[4 + h],
            )
        )

    barrier = pltpu.get_barrier_semaphore()

    def greet(device):
        pl.semaphore_signal(barrier, inc=1, device_id=device, device_id_type=MESH)

    for k in range(1, T):
        greet({"tensor": tensor_peer(k)})
    for k in range(1, S):
        greet({"section": lax.rem(me + k, S)})
    greet({"section": after, "tensor": partner})
    greet({"section": before, "tensor": partner})
    for copy in stage + late:
        copy.start()
    gain_own[...] = jnp.broadcast_to(gain[...].astype(F32), (8, width))
    gain_pair[:, own_half] = gain_own[...]
    pl.semaphore_wait(barrier, T + S)

    for k in range(1, S):
        push(
            audio,
            arecv.at[me],
            w_sems.at[0, 0],
            w_sems.at[1, 0],
            {"section": lax.rem(me + k, S)},
        )
    push(
        gain_own,
        gain_pair.at[:, own_half],
        w_sems.at[0, 1],
        w_sems.at[1, 1],
        {"tensor": partner},
    )
    for h in range(KVH):
        push(
            wkv.at[0, :, lanes(2 * h + 1 - y)],
            w_all.at[own_half, pl.ds(q_cols + h * HD, HD)],
            w_sems.at[0, 3],
            w_sems.at[1, 3],
            {"tensor": partner},
        )
    for k in range(1, Z):
        other = line_peer(k)
        push(
            wq.at[0, pair_rows(other), :],
            w_all.at[:, lanes(z)],
            w_sems.at[0, 4],
            w_sems.at[1, 4],
            {"tensor": other * 2 + y},
        )

    N = dest.shape[1]
    drow = dest[...].astype(F32)
    sub, lane = iota((N, N), 0), iota((N, N), 1)
    dcol = jnp.sum(jnp.where(sub == lane, drow, 0.0), axis=1, keepdims=True)
    same = (dcol == drow) & ((sub >> 5) == (lane >> 5)) & (sub < lane)
    rank = jnp.sum(jnp.where(same, 1.0, 0.0), axis=0, keepdims=True)
    block = (iota((1, N), 1) >> 5).astype(F32)
    slot = block * float(cap) + rank
    mine = drow == me.astype(F32)

    for copy in stage:
        copy.wait()
    drain(arecv.at[pl.ds(0, S - 1)], w_sems.at[1, 0])
    every_row = arecv[...].reshape(N, width)
    for m in range(MB_DEV):
        wanted = (iota((AUD_MB, N), 0) + m * AUD_MB).astype(F32)
        chosen = jnp.where((slot == wanted) & mine, 1.0, 0.0).astype(BF16)
        rows = jnp.dot(chosen, every_row, preferred_element_type=F32)
        xs[0, m, 0:AUD_MB, own_half] = rows.astype(BF16)
        xs[0, m, AUD_MB:MB_ROWS, own_half] = hid[m * TXT_MB : (m + 1) * TXT_MB, :]
        push(
            xs.at[0, m, :, own_half],
            xs.at[0, m, :, own_half],
            w_sems.at[0, 2],
            recv_sems.at[0, m, 5],
            {"tensor": partner},
        )
    for copy in late:
        copy.wait()

    eye = iota((MB_ROWS, MB_ROWS), 0) == iota((MB_ROWS, MB_ROWS), 1)
    causal = iota((MB_ROWS, MB_ROWS), 1) <= iota((MB_ROWS, MB_ROWS), 0)
    scale = 1.0 / math.sqrt(HD)

    def to_col(row):
        return jnp.sum(jnp.where(eye, row, 0.0), axis=1, keepdims=True)

    def to_row(col):
        return jnp.sum(jnp.where(eye, col, 0.0), axis=0, keepdims=True)

    def allowed_of(root, m):
        seg_row = segment[pl.ds(root * MB_DEV + m, 1), :].astype(F32)
        seg_col = to_col(seg_row)
        position = iota((MB_ROWS, N), 0)
        owner = ((position + m * AUD_MB) >> shift).astype(F32)
        named = (drow == root.astype(F32)) & (block == owner)
        count = jnp.sum(jnp.where(named, 1.0, 0.0), axis=1, keepdims=True)
        index = iota((MB_ROWS, 1), 0)
        within = (index & (cap - 1)).astype(F32)
        live = jnp.where((within < count) | (index >= AUD_MB), 1.0, 0.0)
        return causal & (seg_col == seg_row) & ((to_row(live) > 0.5) | eye)

    def project_kv(s, m, first):
        if first:
            drain(xs.at[0, m, :, pl.ds(0, width)], recv_sems.at[0, m, 5])
        else:
            drain(xs.at[s, m], recv_sems.at[s, m, 5])
        x = xs[s, m].astype(F32)
        sums = to_row(jnp.sum(x * x, axis=1, keepdims=True))
        sums = jnp.broadcast_to(sums, (8, MB_ROWS))
        sssend[s, m] = jnp.concatenate([sums, sums], axis=1)
        for k in range(1, Z):
            push(
                sssend.at[s, m],
                ssrecv.at[s, m, k - 1],
                send_sems.at[s, m, 0],
                recv_sems.at[s, m, 0],
                {"tensor": line_peer(k) * 2 + y},
            )
        xg = (x * gain_pair[0:1, :]).astype(BF16)
        if first and m == 0:
            drain(w_all.at[pl.ds(0, width), pl.ds(0, kv_cols)], w_sems.at[1, 3])
        accum[m, :, q_cols:] = jnp.dot(xg, w_all[:, q_cols:], preferred_element_type=F32)
        for k in range(1, Z):
            other = line_peer(k)
            block_of = lanes(Z + lax.div(other, per_kv))
            kvsend[s, m, k - 1] = accum[m, :, block_of].astype(BF16)
            push(
                kvsend.at[s, m, k - 1],
                kvrecv.at[s, m, k - 1],
                send_sems.at[s, m, 2],
                recv_sems.at[s, m, 2],
                {"tensor": other * 2 + y},
            )
        return xg

    def project_q(s, m, first, xg):
        if first and m == 0:
            drain(w_all.at[:, pl.ds(0, (Z - 1) * HD)], w_sems.at[1, 4])
        accum[m, :, :q_cols] = jnp.dot(xg, w_all[:, :q_cols], preferred_element_type=F32)
        for k in range(1, Z):
            other = line_peer(k)
            qsend[s, m, k - 1] = accum[m, :, lanes(other)].astype(BF16)
            push(
                qsend.at[s, m, k - 1],
                qrecv.at[s, m, k - 1],
                send_sems.at[s, m, 1],
                recv_sems.at[s, m, 1],
                {"tensor": other * 2 + y},
            )

    is_key = y == 0

    def swap(s, m):
        drain(ssrecv.at[s, m], recv_sems.at[s, m, 0])
        total = sssend[s, m] + jnp.sum(ssrecv[s, m], axis=0)
        inverse = to_col(lax.rsqrt(total[0:1, 0:MB_ROWS] / D + 1e-05))
        drain(kvrecv.at[s, m], recv_sems.at[s, m, 2])
        arrived = jnp.sum(kvrecv[s, m].astype(F32), axis=0)
        keyval = (accum[m, :, lanes(Z + lax.div(z, per_kv))] + arrived) * inverse
        cos_kv = jnp.where(is_key, cos_ref[...], 1.0)
        sin_kv = jnp.where(is_key, sin_ref[...], 0.0)
        keyval = keyval * cos_kv + pltpu.roll(keyval, HD // 2, 1) * sin_kv
        swsend[s, m] = keyval.astype(BF16)
        push(
            swsend.at[s, m],
            swrecv.at[s, m],
            send_sems.at[s, m, 3],
            recv_sems.at[s, m, 3],
            {"tensor": partner},
        )
        return inverse

    def attend(s, m, inverse, mask):
        drain(qrecv.at[s, m], recv_sems.at[s, m, 1])
        arrived = jnp.sum(qrecv[s, m].astype(F32), axis=0)
        query = (accum[m, :, lanes(z)] + arrived) * inverse
        query = query * cos_ref[...] + pltpu.roll(query, HD // 2, 1) * sin_ref[...]
        drain(swrecv.at[s, m], recv_sems.at[s, m, 3])
        own, got = swsend[s, m], swrecv[s, m]
        keys = jnp.where(is_key, own, got)
        values = jnp.where(is_key, got, own)
        scores = lax.dot_general(
            query.astype(BF16), keys, (((1,), (1,)), ((), ())), preferred_element_type=F32
        )
        scores = jnp.where(mask, scores * scale, -jnp.inf)
        highest = jnp.max(scores, axis=-1, keepdims=True)
        weights = jnp.exp(scores - highest)
        probs = (weights / jnp.sum(weights, axis=-1, keepdims=True)).astype(BF16)
        attended = jnp.dot(probs, values, preferred_element_type=F32)
        att[s, m, :, lanes(t)] = attended.astype(BF16)
        for k in range(1, T):
            push(
                att.at[s, m, :, lanes(t)],
                att.at[s, m, :, lanes(t)],
                send_sems.at[s, m, 4],
                recv_sems.at[s, m, 4],
                {"tensor": tensor_peer(k)},
            )

    def leave(s, m, last):
        drain(att.at[s, m, :, pl.ds(0, (T - 1) * HD)], recv_sems.at[s, m, 4])
        projected = jnp.dot(att[s, m], wo[...], preferred_element_type=F32)
        xnew[s, m] = (xs[s, m, :, own_half].astype(F32) + projected).astype(BF16)
        routes = [{"section": after}]
        if not last:
            routes.append({"section": after, "tensor": partner})
        for route in routes:
            push(
                xnew.at[s, m],
                xs.at[s + 1, m, :, own_half],
                send_sems.at[s, m, 5],
                recv_sems.at[s + 1, m, 5],
                route,
            )

    def step(s, first, last):
        root = lax.rem(me - s + 2 * S, S)
        each = range(MB_DEV)
        if first:
            gained = [project_kv(s, m, first) for m in each]
            masks = [allowed_of(root, m) for m in each]
            inverses = [swap(s, m) for m in each]
            for m in each:
                project_q(s, m, first, gained[m])
        else:
            for m in each:
                project_q(s, m, first, project_kv(s, m, first))
            masks = [allowed_of(root, m) for m in each]
            inverses = [swap(s, m) for m in each]
        for m in range(MB_DEV):
            attend(s, m, inverses[m], masks[m])
        for m in range(MB_DEV):
            leave(s, m, last)

    def middle(s, carry):
        step(s, False, False)
        return carry

    drain(gain_own, w_sems.at[1, 1])
    step(0, True, False)
    lax.fori_loop(1, STEPS - 1, middle, 0)
    step(STEPS - 1, False, True)

    for m in range(MB_DEV):
        drain(xs.at[STEPS, m, :, pl.ds(0, width)], recv_sems.at[STEPS, m, 5])
        out[m * MB_ROWS : (m + 1) * MB_ROWS, :] = xs[STEPS, m, :, own_half]

    drain(arecv.at[pl.ds(0, S - 1)], w_sems.at[0, 0])
    drain(gain_own, w_sems.at[0, 1])
    drain(xs.at[0, :, :, pl.ds(0, width)], w_sems.at[0, 2])
    drain(w_all.at[pl.ds(0, width), pl.ds(0, kv_cols)], w_sems.at[0, 3])
    drain(w_all.at[:, pl.ds(0, (Z - 1) * HD)], w_sems.at[0, 4])

    def finish(s, carry):
        for m in range(MB_DEV):
            drain(ssrecv.at[s, m], send_sems.at[s, m, 0])
            drain(qsend.at[s, m], send_sems.at[s, m, 1])
            drain(kvsend.at[s, m], send_sems.at[s, m, 2])
            drain(swsend.at[s, m], send_sems.at[s, m, 3])
            drain(att.at[s, m, :, pl.ds(0, (T - 1) * HD)], send_sems.at[s, m, 4])
            drain(xnew.at[s, m], send_sems.at[s, m, 5])

            @pl.when(s < STEPS - 1)
            def _():
                drain(xnew.at[s, m], send_sems.at[s, m, 5])

        return carry

    lax.fori_loop(0, STEPS, finish, 0)


def local(S, T, hidden, audio, audio_dest, segment, norm_gain, w_query, w_keyval, w_out):
    width = hidden.shape[1]
    rows = MB_DEV * MB_ROWS
    Z = T // 2
    cols = (Z + KVH) * HD
    cosine, sine = rope_tables()
    vmem = pl.BlockSpec(memory_space=pltpu.VMEM)
    hbm = pl.BlockSpec(memory_space=pl.ANY)
    per = (STEPS, MB_DEV)
    scratch = [
        pltpu.VMEM((2 * width, cols), BF16),
        pltpu.VMEM(w_out.shape[1:], BF16),
        pltpu.VMEM((S, AUD_DEV, width), BF16),
        pltpu.VMEM((MB_DEV * TXT_MB, width), BF16),
        pltpu.VMEM((8, width), F32),
        pltpu.VMEM((8, 2 * width), F32),
        pltpu.VMEM((STEPS + 1, MB_DEV, MB_ROWS, 2 * width), BF16),
        pltpu.VMEM(per + (MB_ROWS, width), BF16),
        pltpu.VMEM((MB_DEV, MB_ROWS, cols), F32),
        pltpu.VMEM(per + (Z - 1, MB_ROWS, HD), BF16),
        pltpu.VMEM(per + (Z - 1, MB_ROWS, HD), BF16),
        pltpu.VMEM(per + (Z - 1, MB_ROWS, HD), BF16),
        pltpu.VMEM(per + (Z - 1, MB_ROWS, HD), BF16),
        pltpu.VMEM(per + (8, 2 * MB_ROWS), F32),
        pltpu.VMEM(per + (Z - 1, 8, 2 * MB_ROWS), F32),
        pltpu.VMEM(per + (MB_ROWS, HD), BF16),
        pltpu.VMEM(per + (MB_ROWS, HD), BF16),
        pltpu.VMEM(per + (MB_ROWS, T * HD), BF16),
        pltpu.SemaphoreType.DMA((4 + KVH,)),
        pltpu.SemaphoreType.DMA((2, 5)),
        pltpu.SemaphoreType.DMA(per + (6,)),
        pltpu.SemaphoreType.DMA((STEPS + 1, MB_DEV, 6)),
    ]
    return pl.pallas_call(
        functools.partial(kernel, S, T),
        out_shape=jax.ShapeDtypeStruct((rows, width), BF16),
        in_specs=[hbm, hbm, vmem, vmem, vmem, hbm, hbm, hbm, vmem, vmem],
        out_specs=vmem,
        scratch_shapes=scratch,
        compiler_params=pltpu.CompilerParams(
            collective_id=0, has_side_effects=True, vmem_limit_bytes=62 * 1024 * 1024
        ),
        cost_estimate=pl.CostEstimate(
            flops=STEPS * rows * width * (2 * cols + T * HD) * 2,
            bytes_accessed=8 * 1024 * 1024,
            transcendentals=0,
        ),
    )(
        hidden,
        audio,
        audio_dest.reshape(1, -1),
        segment,
        norm_gain,
        w_query,
        w_keyval,
        w_out,
        jnp.asarray(cosine),
        jnp.asarray(sine),
    )


def solution(mesh):
    in_specs = (
        P("section", "tensor"),
        P("section", "tensor"),
        P(),
        P(),
        P("section", "tensor"),
        P("section", None, "tensor"),
        P("section", "tensor", None),
        P("section", None, "tensor"),
    )
    out_specs = P("section", "tensor")
    body = functools.partial(local, mesh.shape["section"], mesh.shape["tensor"])
    return jax.shard_map(body, mesh=mesh, in_specs=in_specs, out_specs=out_specs, check_vma=False)
```

time: 154 us -> 130 us (0.84)
  Pallas kernels: 144 us -> 128 us
  local copies, waits for them, and re-layouts: 9.27 us -> 1.67 us
    pallas_call x1, Pallas kernels: 144 us -> 128 us  [local(): pl.pallas_call(functools.partial(kernel, S, T), out_shape=jax.ShapeDtypeS...]
    unnamed x18 -> x1, local copies, waits for them, and re-layouts: 9.27 us -> 1.67 us
where the time goes in v2:
time: 130 us
  Pallas kernels  128 us (98%)
  local copies, waits for them, and re-layouts  1.67 us (1%)
    pallas_call x1, Pallas kernels, local(): pl.pallas_call(functools.partial(kernel, S, T), out_shape=jax.ShapeDtypeS...  128 us

profile of v2, /device:TPU:0, one launch (start us, length us, event | category | flops | bytes accessed | tf_op | source)
XLA Modules:
  0.0 129.8 jit_solution(7053188111573139650)
XLA Ops:
  0.0 128.2 %shard_map.100 = bf16[128,1024]{1,0:T(8,128)(2,1)} custom-call(bf16[64,1024]{1,0:T(8,128)(2,1)} %hidden.1, bf16[32,1024]{1,0:T(8,128)(2,1)} %audio.1, s32[1,128]{1,0:T(1,128)} %bitcast.1, s32[8,64]{1,0:T(8,128)} %segment.1, bf16[1,1024]{1,0:T(2,128)(2,1)} %gain.1, bf16[1,8192,128]{2,1,0:T(8,128)(2,1)} %wq.1, bf16[1,1024,1024]{2,1,0:T(8,128)(2,1)} %wkv.1, ...), custom_call_target="tpu_custom_call" | custom-call | flops 3221225472 | bytes 8388608 | tf_op jit(solution)/shard_map/pallas_call | solution.py:444
  128.2 1.7 %copy.12 = bf16[128,1024]{1,0:T(8,128)(2,1)} copy(bf16[128,1024]{1,0:T(8,128)(2,1)} %shard_map.100) | data formatting | bytes 524288

commit v3 on v2

--- a/solution.py
+++ b/solution.py
@@ -58,11 +58,13 @@
     out,
     w_all,
     wo,
+    wo_before,
     arecv,
     hid,
     gain_own,
     gain_pair,
     xs,
+    xold,
     xnew,
     accum,
     qsend,
@@ -74,6 +76,7 @@
     swsend,
     swrecv,
     att,
+    attsend,
     local_sem,
     w_sems,
     send_sems,
@@ -145,13 +148,14 @@
         greet({"tensor": tensor_peer(k)})
     for k in range(1, S):
         greet({"section": lax.rem(me + k, S)})
-    greet({"section": after, "tensor": partner})
-    greet({"section": before, "tensor": partner})
+    for k in range(1, T):
+        greet({"section": after, "tensor": tensor_peer(k)})
+        greet({"section": before, "tensor": tensor_peer(k)})
     for copy in stage + late:
         copy.start()
     gain_own[...] = jnp.broadcast_to(gain[...].astype(F32), (8, width))
     gain_pair[:, own_half] = gain_own[...]
-    pl.semaphore_wait(barrier, T + S)
+    pl.semaphore_wait(barrier, 3 * (T - 1) + S - 1)
 
     for k in range(1, S):
         push(
@@ -184,6 +188,15 @@
             w_sems.at[0, 4],
             w_sems.at[1, 4],
             {"tensor": other * 2 + y},
+        )
+
+    for target in (t, partner):
+        push(
+            wo_hbm.at[0],
+            wo_before.at[:, own_half],
+            w_sems.at[0, 5],
+            w_sems.at[1, 5],
+            {"section": after, "tensor": target},
         )
 
     N = dest.shape[1]
@@ -238,12 +251,33 @@
         live = jnp.where((within < count) | (index >= AUD_MB), 1.0, 0.0)
         return causal & (seg_col == seg_row) & ((to_row(live) > 0.5) | eye)
 
+    def arrive(s, m, columns):
+        if s == 2 and m == 0:
+            drain(wo_before, w_sems.at[1, 5])
+        drain(xold.at[s, m], recv_sems.at[s, m, 5])
+        drain(att.at[s - 1, m], recv_sems.at[s - 1, m, 4])
+        projected = jnp.dot(att[s - 1, m], wo_before[:, columns], preferred_element_type=F32)
+        return xold[s, m, :, columns].astype(F32) + projected
+
     def project_kv(s, m, first):
         if first:
             drain(xs.at[0, m, :, pl.ds(0, width)], recv_sems.at[0, m, 5])
+            x = xs[s, m].astype(F32)
+        elif s == 1:
+            drain(xs.at[s, m], recv_sems.at[s, m, 5])
+            x = xs[s, m].astype(F32)
         else:
-            drain(xs.at[s, m], recv_sems.at[s, m, 5])
-        x = xs[s, m].astype(F32)
+            x = arrive(s, m, slice(None)).astype(BF16)
+            xs[s, m] = x
+            x = x.astype(F32)
+        if not first:
+            push(
+                xs.at[s, m],
+                xold.at[s + 1, m],
+                send_sems.at[s, m, 5],
+                recv_sems.at[s + 1, m, 5],
+                {"section": after},
+            )
         sums = to_row(jnp.sum(x * x, axis=1, keepdims=True))
         sums = jnp.broadcast_to(sums, (8, MB_ROWS))
         sssend[s, m] = jnp.concatenate([sums, sums], axis=1)
@@ -326,6 +360,17 @@
         weights = jnp.exp(scores - highest)
         probs = (weights / jnp.sum(weights, axis=-1, keepdims=True)).astype(BF16)
         attended = jnp.dot(probs, values, preferred_element_type=F32)
+        if s > 0:
+            attsend[s, m] = attended.astype(BF16)
+            for k in range(T):
+                push(
+                    attsend.at[s, m],
+                    att.at[s, m, :, lanes(t)],
+                    send_sems.at[s, m, 4],
+                    recv_sems.at[s, m, 4],
+                    {"section": after, "tensor": tensor_peer(k)},
+                )
+            return
         att[s, m, :, lanes(t)] = attended.astype(BF16)
         for k in range(1, T):
             push(
@@ -336,23 +381,20 @@
                 {"tensor": tensor_peer(k)},
             )
 
-    def leave(s, m, last):
+    def leave(s, m):
         drain(att.at[s, m, :, pl.ds(0, (T - 1) * HD)], recv_sems.at[s, m, 4])
         projected = jnp.dot(att[s, m], wo[...], preferred_element_type=F32)
-        xnew[s, m] = (xs[s, m, :, own_half].astype(F32) + projected).astype(BF16)
-        routes = [{"section": after}]
-        if not last:
-            routes.append({"section": after, "tensor": partner})
-        for route in routes:
+        xnew[m] = (xs[s, m, :, own_half].astype(F32) + projected).astype(BF16)
+        for target in (t, partner):
             push(
-                xnew.at[s, m],
+                xnew.at[m],
                 xs.at[s + 1, m, :, own_half],
                 send_sems.at[s, m, 5],
                 recv_sems.at[s + 1, m, 5],
-                route,
-            )
-
-    def step(s, first, last):
+                {"section": after, "tensor": target},
+            )
+
+    def step(s, first):
         root = lax.rem(me - s + 2 * S, S)
         each = range(MB_DEV)
         if first:
@@ -368,21 +410,15 @@
             inverses = [swap(s, m) for m in each]
         for m in range(MB_DEV):
             attend(s, m, inverses[m], masks[m])
-        for m in range(MB_DEV):
-            leave(s, m, last)
-
-    def middle(s, carry):
-        step(s, False, False)
-        return carry
+        if first:
+            for m in each:
+                leave(s, m)
 
     drain(gain_own, w_sems.at[1, 1])
-    step(0, True, False)
-    lax.fori_loop(1, STEPS - 1, middle, 0)
-    step(STEPS - 1, False, True)
-
+    for s in range(STEPS):
+        step(s, s == 0)
     for m in range(MB_DEV):
-        drain(xs.at[STEPS, m, :, pl.ds(0, width)], recv_sems.at[STEPS, m, 5])
-        out[m * MB_ROWS : (m + 1) * MB_ROWS, :] = xs[STEPS, m, :, own_half]
+        out[m * MB_ROWS : (m + 1) * MB_ROWS, :] = arrive(STEPS, m, own_half).astype(BF16)
 
     drain(arecv.at[pl.ds(0, S - 1)], w_sems.at[0, 0])
     drain(gain_own, w_sems.at[0, 1])
@@ -390,22 +426,16 @@
     drain(w_all.at[pl.ds(0, width), pl.ds(0, kv_cols)], w_sems.at[0, 3])
     drain(w_all.at[:, pl.ds(0, (Z - 1) * HD)], w_sems.at[0, 4])
 
-    def finish(s, carry):
+    drain(wo_before, w_sems.at[0, 5])
+    for s in range(STEPS):
         for m in range(MB_DEV):
             drain(ssrecv.at[s, m], send_sems.at[s, m, 0])
             drain(qsend.at[s, m], send_sems.at[s, m, 1])
             drain(kvsend.at[s, m], send_sems.at[s, m, 2])
             drain(swsend.at[s, m], send_sems.at[s, m, 3])
-            drain(att.at[s, m, :, pl.ds(0, (T - 1) * HD)], send_sems.at[s, m, 4])
-            drain(xnew.at[s, m], send_sems.at[s, m, 5])
-
-            @pl.when(s < STEPS - 1)
-            def _():
-                drain(xnew.at[s, m], send_sems.at[s, m, 5])
-
-        return carry
-
-    lax.fori_loop(0, STEPS, finish, 0)
+            sent = T if s > 0 else T - 1
+            drain(att.at[s, m, :, pl.ds(0, sent * HD)], send_sems.at[s, m, 4])
+            drain(xs.at[s, m], send_sems.at[s, m, 5])
 
 
 def local(S, T, hidden, audio, audio_dest, segment, norm_gain, w_query, w_keyval, w_out):
@@ -420,12 +450,14 @@
     scratch = [
         pltpu.VMEM((2 * width, cols), BF16),
         pltpu.VMEM(w_out.shape[1:], BF16),
+        pltpu.VMEM((T * HD, 2 * width), BF16),
         pltpu.VMEM((S, AUD_DEV, width), BF16),
         pltpu.VMEM((MB_DEV * TXT_MB, width), BF16),
         pltpu.VMEM((8, width), F32),
         pltpu.VMEM((8, 2 * width), F32),
+        pltpu.VMEM(per + (MB_ROWS, 2 * width), BF16),
         pltpu.VMEM((STEPS + 1, MB_DEV, MB_ROWS, 2 * width), BF16),
-        pltpu.VMEM(per + (MB_ROWS, width), BF16),
+        pltpu.VMEM((MB_DEV, MB_ROWS, width), BF16),
         pltpu.VMEM((MB_DEV, MB_ROWS, cols), F32),
         pltpu.VMEM(per + (Z - 1, MB_ROWS, HD), BF16),
         pltpu.VMEM(per + (Z - 1, MB_ROWS, HD), BF16),
@@ -436,8 +468,9 @@
         pltpu.VMEM(per + (MB_ROWS, HD), BF16),
         pltpu.VMEM(per + (MB_ROWS, HD), BF16),
         pltpu.VMEM(per + (MB_ROWS, T * HD), BF16),
+        pltpu.VMEM(per + (MB_ROWS, HD), BF16),
         pltpu.SemaphoreType.DMA((4 + KVH,)),
-        pltpu.SemaphoreType.DMA((2, 5)),
+        pltpu.SemaphoreType.DMA((2, 6)),
         pltpu.SemaphoreType.DMA(per + (6,)),
         pltpu.SemaphoreType.DMA((STEPS + 1, MB_DEV, 6)),
     ]

time: 130 us -> 152 us (1.17)
  Pallas kernels: 128 us -> 150 us
    pallas_call x1, Pallas kernels: 128 us -> 150 us  [local(): pl.pallas_call(functools.partial(kernel, S, T), out_shape=jax.ShapeDtypeS...]
where the time goes in v3:
time: 152 us
  Pallas kernels  150 us (99%)
  local copies, waits for them, and re-layouts  1.67 us (1%)
    pallas_call x1, Pallas kernels, local(): pl.pallas_call(functools.partial(kernel, S, T), out_shape=jax.ShapeDtypeS...  150 us

profile of v3, /device:TPU:0, one launch (start us, length us, event | category | flops | bytes accessed | tf_op | source)
XLA Modules:
  0.0 152.0 jit_solution(3511571198876833360)
XLA Ops:
  0.0 150.3 %shard_map.100 = bf16[128,1024]{1,0:T(8,128)(2,1)} custom-call(bf16[64,1024]{1,0:T(8,128)(2,1)} %hidden.1, bf16[32,1024]{1,0:T(8,128)(2,1)} %audio.1, s32[1,128]{1,0:T(1,128)} %bitcast.1, s32[8,64]{1,0:T(8,128)} %segment.1, bf16[1,1024]{1,0:T(2,128)(2,1)} %gain.1, bf16[1,8192,128]{2,1,0:T(8,128)(2,1)} %wq.1, bf16[1,1024,1024]{2,1,0:T(8,128)(2,1)} %wkv.1, ...), custom_call_target="tpu_custom_call" | custom-call | flops 3221225472 | bytes 8388608 | tf_op jit(solution)/shard_map/pallas_call | solution.py:477
  150.3 1.7 %copy.12 = bf16[128,1024]{1,0:T(8,128)(2,1)} copy(bf16[128,1024]{1,0:T(8,128)(2,1)} %shard_map.100) | data formatting | bytes 524288

commit v4 on v3

--- a/solution.py
+++ b/solution.py
@@ -17,7 +17,9 @@
 TXT_MB = 32
 AUD_DEV = 32
 STEPS = 4
+DIRECT = 3
 MB_ROWS = 64
+SQ_ROWS = 16
 MESH = pl.DeviceIdType.MESH
 F32 = jnp.float32
 BF16 = jnp.bfloat16
@@ -71,8 +73,6 @@
     qrecv,
     kvsend,
     kvrecv,
-    sssend,
-    ssrecv,
     swsend,
     swrecv,
     att,
@@ -190,10 +190,10 @@
             {"tensor": other * 2 + y},
         )
 
-    for target in (t, partner):
+    for target in (t,) if DIRECT == STEPS - 1 else (t, partner):
         push(
             wo_hbm.at[0],
-            wo_before.at[:, own_half],
+            wo_before if DIRECT == STEPS - 1 else wo_before.at[:, own_half],
             w_sems.at[0, 5],
             w_sems.at[1, 5],
             {"section": after, "tensor": target},
@@ -252,43 +252,42 @@
         return causal & (seg_col == seg_row) & ((to_row(live) > 0.5) | eye)
 
     def arrive(s, m, columns):
-        if s == 2 and m == 0:
+        if s == DIRECT + 1 and m == 0:
             drain(wo_before, w_sems.at[1, 5])
-        drain(xold.at[s, m], recv_sems.at[s, m, 5])
+        drain(xold.at[s, m, :, pl.ds(0, width if s == STEPS else 2 * width)], recv_sems.at[s, m, 5])
         drain(att.at[s - 1, m], recv_sems.at[s - 1, m, 4])
-        projected = jnp.dot(att[s - 1, m], wo_before[:, columns], preferred_element_type=F32)
+        projected = jnp.dot(
+            att[s - 1, m],
+            wo_before[...] if DIRECT == STEPS - 1 else wo_before[:, columns],
+            preferred_element_type=F32,
+        )
         return xold[s, m, :, columns].astype(F32) + projected
 
     def project_kv(s, m, first):
         if first:
             drain(xs.at[0, m, :, pl.ds(0, width)], recv_sems.at[0, m, 5])
             x = xs[s, m].astype(F32)
-        elif s == 1:
+        elif s <= DIRECT:
             drain(xs.at[s, m], recv_sems.at[s, m, 5])
             x = xs[s, m].astype(F32)
         else:
             x = arrive(s, m, slice(None)).astype(BF16)
             xs[s, m] = x
             x = x.astype(F32)
-        if not first:
+        if s >= DIRECT:
+            wanted = own_half if s == STEPS - 1 else slice(None)
             push(
-                xs.at[s, m],
-                xold.at[s + 1, m],
+                xs.at[s, m, :, wanted],
+                xold.at[s + 1, m, :, wanted],
                 send_sems.at[s, m, 5],
                 recv_sems.at[s + 1, m, 5],
                 {"section": after},
             )
         sums = to_row(jnp.sum(x * x, axis=1, keepdims=True))
-        sums = jnp.broadcast_to(sums, (8, MB_ROWS))
-        sssend[s, m] = jnp.concatenate([sums, sums], axis=1)
-        for k in range(1, Z):
-            push(
-                sssend.at[s, m],
-                ssrecv.at[s, m, k - 1],
-                send_sems.at[s, m, 0],
-                recv_sems.at[s, m, 0],
-                {"tensor": line_peer(k) * 2 + y},
-            )
+        both = jnp.concatenate([sums, sums], axis=1)
+        high = both.astype(BF16).astype(F32)
+        place = iota((SQ_ROWS, HD), 0)
+        squares = jnp.where(place == 0, high, jnp.where(place == 1, both - high, 0.0)).astype(BF16)
         xg = (x * gain_pair[0:1, :]).astype(BF16)
         if first and m == 0:
             drain(w_all.at[pl.ds(0, width), pl.ds(0, kv_cols)], w_sems.at[1, 3])
@@ -296,7 +295,8 @@
         for k in range(1, Z):
             other = line_peer(k)
             block_of = lanes(Z + lax.div(other, per_kv))
-            kvsend[s, m, k - 1] = accum[m, :, block_of].astype(BF16)
+            kvsend[s, m, k - 1, 0:MB_ROWS, :] = accum[m, :, block_of].astype(BF16)
+            kvsend[s, m, k - 1, MB_ROWS:, :] = squares
             push(
                 kvsend.at[s, m, k - 1],
                 kvrecv.at[s, m, k - 1],
@@ -304,7 +304,7 @@
                 recv_sems.at[s, m, 2],
                 {"tensor": other * 2 + y},
             )
-        return xg
+        return xg, sums
 
     def project_q(s, m, first, xg):
         if first and m == 0:
@@ -323,13 +323,14 @@
 
     is_key = y == 0
 
-    def swap(s, m):
-        drain(ssrecv.at[s, m], recv_sems.at[s, m, 0])
-        total = sssend[s, m] + jnp.sum(ssrecv[s, m], axis=0)
-        inverse = to_col(lax.rsqrt(total[0:1, 0:MB_ROWS] / D + 1e-05))
+    def swap(s, m, sums):
         drain(kvrecv.at[s, m], recv_sems.at[s, m, 2])
         arrived = jnp.sum(kvrecv[s, m].astype(F32), axis=0)
-        keyval = (accum[m, :, lanes(Z + lax.div(z, per_kv))] + arrived) * inverse
+        squares = arrived[MB_ROWS : MB_ROWS + 1, 0:MB_ROWS]
+        squares = squares + arrived[MB_ROWS + 1 : MB_ROWS + 2, 0:MB_ROWS]
+        inverse = to_col(lax.rsqrt((sums + squares) / D + 1e-05))
+        keyval = accum[m, :, lanes(Z + lax.div(z, per_kv))] + arrived[0:MB_ROWS]
+        keyval = keyval * inverse
         cos_kv = jnp.where(is_key, cos_ref[...], 1.0)
         sin_kv = jnp.where(is_key, sin_ref[...], 0.0)
         keyval = keyval * cos_kv + pltpu.roll(keyval, HD // 2, 1) * sin_kv
@@ -360,7 +361,7 @@
         weights = jnp.exp(scores - highest)
         probs = (weights / jnp.sum(weights, axis=-1, keepdims=True)).astype(BF16)
         attended = jnp.dot(probs, values, preferred_element_type=F32)
-        if s > 0:
+        if s >= DIRECT:
             attsend[s, m] = attended.astype(BF16)
             for k in range(T):
                 push(
@@ -384,10 +385,10 @@
     def leave(s, m):
         drain(att.at[s, m, :, pl.ds(0, (T - 1) * HD)], recv_sems.at[s, m, 4])
         projected = jnp.dot(att[s, m], wo[...], preferred_element_type=F32)
-        xnew[m] = (xs[s, m, :, own_half].astype(F32) + projected).astype(BF16)
+        xnew[s, m] = (xs[s, m, :, own_half].astype(F32) + projected).astype(BF16)
         for target in (t, partner):
             push(
-                xnew.at[m],
+                xnew.at[s, m],
                 xs.at[s + 1, m, :, own_half],
                 send_sems.at[s, m, 5],
                 recv_sems.at[s + 1, m, 5],
@@ -397,20 +398,19 @@
     def step(s, first):
         root = lax.rem(me - s + 2 * S, S)
         each = range(MB_DEV)
+        gained = []
+        for m in each:
+            gained.append(project_kv(s, m, first))
+            if not first:
+                project_q(s, m, first, gained[m][0])
+        masks = [allowed_of(root, m) for m in each]
+        inverses = [swap(s, m, gained[m][1]) for m in each]
         if first:
-            gained = [project_kv(s, m, first) for m in each]
-            masks = [allowed_of(root, m) for m in each]
-            inverses = [swap(s, m) for m in each]
             for m in each:
-                project_q(s, m, first, gained[m])
-        else:
-            for m in each:
-                project_q(s, m, first, project_kv(s, m, first))
-            masks = [allowed_of(root, m) for m in each]
-            inverses = [swap(s, m) for m in each]
+                project_q(s, m, first, gained[m][0])
         for m in range(MB_DEV):
             attend(s, m, inverses[m], masks[m])
-        if first:
+        if s < DIRECT:
             for m in each:
                 leave(s, m)
 
@@ -429,13 +429,13 @@
     drain(wo_before, w_sems.at[0, 5])
     for s in range(STEPS):
         for m in range(MB_DEV):
-            drain(ssrecv.at[s, m], send_sems.at[s, m, 0])
             drain(qsend.at[s, m], send_sems.at[s, m, 1])
             drain(kvsend.at[s, m], send_sems.at[s, m, 2])
             drain(swsend.at[s, m], send_sems.at[s, m, 3])
-            sent = T if s > 0 else T - 1
+            sent = T if s >= DIRECT else T - 1
             drain(att.at[s, m, :, pl.ds(0, sent * HD)], send_sems.at[s, m, 4])
-            drain(xs.at[s, m], send_sems.at[s, m, 5])
+            sent = width if s == STEPS - 1 else 2 * width
+            drain(xs.at[s, m, :, pl.ds(0, sent)], send_sems.at[s, m, 5])
 
 
 def local(S, T, hidden, audio, audio_dest, segment, norm_gain, w_query, w_keyval, w_out):
@@ -450,21 +450,19 @@
     scratch = [
         pltpu.VMEM((2 * width, cols), BF16),
         pltpu.VMEM(w_out.shape[1:], BF16),
-        pltpu.VMEM((T * HD, 2 * width), BF16),
+        pltpu.VMEM((T * HD, width if DIRECT == STEPS - 1 else 2 * width), BF16),
         pltpu.VMEM((S, AUD_DEV, width), BF16),
         pltpu.VMEM((MB_DEV * TXT_MB, width), BF16),
         pltpu.VMEM((8, width), F32),
         pltpu.VMEM((8, 2 * width), F32),
         pltpu.VMEM(per + (MB_ROWS, 2 * width), BF16),
         pltpu.VMEM((STEPS + 1, MB_DEV, MB_ROWS, 2 * width), BF16),
-        pltpu.VMEM((MB_DEV, MB_ROWS, width), BF16),
+        pltpu.VMEM(per + (MB_ROWS, width), BF16),
         pltpu.VMEM((MB_DEV, MB_ROWS, cols), F32),
         pltpu.VMEM(per + (Z - 1, MB_ROWS, HD), BF16),
         pltpu.VMEM(per + (Z - 1, MB_ROWS, HD), BF16),
-        pltpu.VMEM(per + (Z - 1, MB_ROWS, HD), BF16),
-        pltpu.VMEM(per + (Z - 1, MB_ROWS, HD), BF16),
-        pltpu.VMEM(per + (8, 2 * MB_ROWS), F32),
-        pltpu.VMEM(per + (Z - 1, 8, 2 * MB_ROWS), F32),
+        pltpu.VMEM(per + (Z - 1, MB_ROWS + SQ_ROWS, HD), BF16),
+        pltpu.VMEM(per + (Z - 1, MB_ROWS + SQ_ROWS, HD), BF16),
         pltpu.VMEM(per + (MB_ROWS, HD), BF16),
         pltpu.VMEM(per + (MB_ROWS, HD), BF16),
         pltpu.VMEM(per + (MB_ROWS, T * HD), BF16),

time: 152 us -> 131 us (0.86)
  Pallas kernels: 150 us -> 129 us
    pallas_call x1, Pallas kernels: 150 us -> 129 us  [local(): pl.pallas_call(functools.partial(kernel, S, T), out_shape=jax.ShapeDtypeS...]
where the time goes in v4:
time: 131 us
  Pallas kernels  129 us (98%)
  local copies, waits for them, and re-layouts  1.67 us (1%)
    pallas_call x1, Pallas kernels, local(): pl.pallas_call(functools.partial(kernel, S, T), out_shape=jax.ShapeDtypeS...  129 us

profile of v4, /device:TPU:0, one launch (start us, length us, event | category | flops | bytes accessed | tf_op | source)
XLA Modules:
  0.0 130.7 jit_solution(10143356521654716077)
XLA Ops:
  0.0 129.0 %shard_map.100 = bf16[128,1024]{1,0:T(8,128)(2,1)} custom-call(bf16[64,1024]{1,0:T(8,128)(2,1)} %hidden.1, bf16[32,1024]{1,0:T(8,128)(2,1)} %audio.1, s32[1,128]{1,0:T(1,128)} %bitcast.1, s32[8,64]{1,0:T(8,128)} %segment.1, bf16[1,1024]{1,0:T(2,128)(2,1)} %gain.1, bf16[1,8192,128]{2,1,0:T(8,128)(2,1)} %wq.1, bf16[1,1024,1024]{2,1,0:T(8,128)(2,1)} %wkv.1, ...), custom_call_target="tpu_custom_call" | custom-call | flops 3221225472 | bytes 8388608 | tf_op jit(solution)/shard_map/pallas_call | solution.py:475
  129.1 1.7 %copy.12 = bf16[128,1024]{1,0:T(8,128)(2,1)} copy(bf16[128,1024]{1,0:T(8,128)(2,1)} %shard_map.100) | data formatting | bytes 524288

commit v5 on v4

--- a/solution.py
+++ b/solution.py
@@ -172,7 +172,18 @@
         w_sems.at[1, 1],
         {"tensor": partner},
     )
+    piece = 2 * width // KVH
     for h in range(KVH):
+        for k in range(1, Z):
+            other = line_peer(k)
+            begin = other * 2 * width + h * piece
+            push(
+                wq.at[0, pl.ds(pl.multiple_of(begin, piece), piece), :],
+                w_all.at[pl.ds(h * piece, piece), lanes(z)],
+                w_sems.at[0, 4],
+                w_sems.at[1, 4],
+                {"tensor": other * 2 + y},
+            )
         push(
             wkv.at[0, :, lanes(2 * h + 1 - y)],
             w_all.at[own_half, pl.ds(q_cols + h * HD, HD)],
@@ -180,24 +191,19 @@
             w_sems.at[1, 3],
             {"tensor": partner},
         )
-    for k in range(1, Z):
-        other = line_peer(k)
-        push(
-            wq.at[0, pair_rows(other), :],
-            w_all.at[:, lanes(z)],
-            w_sems.at[0, 4],
-            w_sems.at[1, 4],
-            {"tensor": other * 2 + y},
-        )
-
-    for target in (t,) if DIRECT == STEPS - 1 else (t, partner):
-        push(
-            wo_hbm.at[0],
-            wo_before if DIRECT == STEPS - 1 else wo_before.at[:, own_half],
-            w_sems.at[0, 5],
-            w_sems.at[1, 5],
-            {"section": after, "tensor": target},
-        )
+
+    out_piece = T * HD // 8
+
+    def push_out_rows(first_piece, count):
+        for i in range(first_piece, first_piece + count):
+            rows_of = pl.ds(i * out_piece, out_piece)
+            push(
+                wo_hbm.at[0, rows_of, :],
+                wo_before.at[rows_of, :],
+                w_sems.at[0, 5],
+                w_sems.at[1, 5],
+                {"section": after},
+            )
 
     N = dest.shape[1]
     drow = dest[...].astype(F32)
@@ -408,11 +414,19 @@
         if first:
             for m in each:
                 project_q(s, m, first, gained[m][0])
-        for m in range(MB_DEV):
+        spread = s in (DIRECT - 2, DIRECT - 1)
+        done = 4 * (s - DIRECT + 2)
+        if spread:
+            push_out_rows(done, 1)
+        for m in each:
             attend(s, m, inverses[m], masks[m])
+        if spread:
+            push_out_rows(done + 1, 2)
         if s < DIRECT:
             for m in each:
                 leave(s, m)
+        if spread:
+            push_out_rows(done + 3, 1)
 
     drain(gain_own, w_sems.at[1, 1])
     for s in range(STEPS):

time: 131 us -> 133 us (1.015)
  no operation moved by 1% of the time
where the time goes in v5:
time: 133 us; the launch traced here: 132 us
  Pallas kernels  130 us (98%)
  local copies, waits for them, and re-layouts  1.67 us (1%)
    pallas_call x1, Pallas kernels, local(): pl.pallas_call(functools.partial(kernel, S, T), out_shape=jax.ShapeDtypeS...  130 us

profile of v5, /device:TPU:0, one launch (start us, length us, event | category | flops | bytes accessed | tf_op | source)
XLA Modules:
  0.0 132.0 jit_solution(11216897601571663987)
XLA Ops:
  0.0 130.4 %shard_map.100 = bf16[128,1024]{1,0:T(8,128)(2,1)} custom-call(bf16[64,1024]{1,0:T(8,128)(2,1)} %hidden.1, bf16[32,1024]{1,0:T(8,128)(2,1)} %audio.1, s32[1,128]{1,0:T(1,128)} %bitcast.1, s32[8,64]{1,0:T(8,128)} %segment.1, bf16[1,1024]{1,0:T(2,128)(2,1)} %gain.1, bf16[1,8192,128]{2,1,0:T(8,128)(2,1)} %wq.1, bf16[1,1024,1024]{2,1,0:T(8,128)(2,1)} %wkv.1, ...), custom_call_target="tpu_custom_call" | custom-call | flops 3221225472 | bytes 8388608 | tf_op jit(solution)/shard_map/pallas_call | solution.py:489
  130.4 1.7 %copy.12 = bf16[128,1024]{1,0:T(8,128)(2,1)} copy(bf16[128,1024]{1,0:T(8,128)(2,1)} %shard_map.100) | data formatting | bytes 524288

commit v6 on v2

--- a/solution.py
+++ b/solution.py
@@ -18,6 +18,7 @@
 AUD_DEV = 32
 STEPS = 4
 MB_ROWS = 64
+SQ_ROWS = 16
 MESH = pl.DeviceIdType.MESH
 F32 = jnp.float32
 BF16 = jnp.bfloat16
@@ -69,11 +70,13 @@
     qrecv,
     kvsend,
     kvrecv,
-    sssend,
-    ssrecv,
     swsend,
     swrecv,
     att,
+    xgain,
+    squares_own,
+    inverses,
+    masks,
     local_sem,
     w_sems,
     send_sems,
@@ -238,31 +241,33 @@
         live = jnp.where((within < count) | (index >= AUD_MB), 1.0, 0.0)
         return causal & (seg_col == seg_row) & ((to_row(live) > 0.5) | eye)
 
-    def project_kv(s, m, first):
-        if first:
+    def project_kv(s, m):
+        @pl.when(s == 0)
+        def _():
             drain(xs.at[0, m, :, pl.ds(0, width)], recv_sems.at[0, m, 5])
-        else:
+
+        @pl.when(s > 0)
+        def _():
             drain(xs.at[s, m], recv_sems.at[s, m, 5])
+
         x = xs[s, m].astype(F32)
         sums = to_row(jnp.sum(x * x, axis=1, keepdims=True))
-        sums = jnp.broadcast_to(sums, (8, MB_ROWS))
-        sssend[s, m] = jnp.concatenate([sums, sums], axis=1)
-        for k in range(1, Z):
-            push(
-                sssend.at[s, m],
-                ssrecv.at[s, m, k - 1],
-                send_sems.at[s, m, 0],
-                recv_sems.at[s, m, 0],
-                {"tensor": line_peer(k) * 2 + y},
-            )
-        xg = (x * gain_pair[0:1, :]).astype(BF16)
-        if first and m == 0:
+        both = jnp.concatenate([sums, sums], axis=1)
+        high = both.astype(BF16).astype(F32)
+        place = iota((SQ_ROWS, HD), 0)
+        squares = jnp.where(place == 0, high, jnp.where(place == 1, both - high, 0.0)).astype(BF16)
+        squares_own[m] = jnp.broadcast_to(both, (8, HD))
+        xgain[m] = (x * gain_pair[0:1, :]).astype(BF16)
+
+        @pl.when((s == 0) & (m == 0))
+        def _():
             drain(w_all.at[pl.ds(0, width), pl.ds(0, kv_cols)], w_sems.at[1, 3])
-        accum[m, :, q_cols:] = jnp.dot(xg, w_all[:, q_cols:], preferred_element_type=F32)
+        accum[m, :, q_cols:] = jnp.dot(xgain[m], w_all[:, q_cols:], preferred_element_type=F32)
         for k in range(1, Z):
             other = line_peer(k)
             block_of = lanes(Z + lax.div(other, per_kv))
-            kvsend[s, m, k - 1] = accum[m, :, block_of].astype(BF16)
+            kvsend[s, m, k - 1, 0:MB_ROWS, :] = accum[m, :, block_of].astype(BF16)
+            kvsend[s, m, k - 1, MB_ROWS:, :] = squares
             push(
                 kvsend.at[s, m, k - 1],
                 kvrecv.at[s, m, k - 1],
@@ -270,12 +275,12 @@
                 recv_sems.at[s, m, 2],
                 {"tensor": other * 2 + y},
             )
-        return xg
-
-    def project_q(s, m, first, xg):
-        if first and m == 0:
+
+    def project_q(s, m):
+        @pl.when((s == 0) & (m == 0))
+        def _():
             drain(w_all.at[:, pl.ds(0, (Z - 1) * HD)], w_sems.at[1, 4])
-        accum[m, :, :q_cols] = jnp.dot(xg, w_all[:, :q_cols], preferred_element_type=F32)
+        accum[m, :, :q_cols] = jnp.dot(xgain[m], w_all[:, :q_cols], preferred_element_type=F32)
         for k in range(1, Z):
             other = line_peer(k)
             qsend[s, m, k - 1] = accum[m, :, lanes(other)].astype(BF16)
@@ -290,12 +295,13 @@
     is_key = y == 0
 
     def swap(s, m):
-        drain(ssrecv.at[s, m], recv_sems.at[s, m, 0])
-        total = sssend[s, m] + jnp.sum(ssrecv[s, m], axis=0)
-        inverse = to_col(lax.rsqrt(total[0:1, 0:MB_ROWS] / D + 1e-05))
         drain(kvrecv.at[s, m], recv_sems.at[s, m, 2])
         arrived = jnp.sum(kvrecv[s, m].astype(F32), axis=0)
-        keyval = (accum[m, :, lanes(Z + lax.div(z, per_kv))] + arrived) * inverse
+        squares = arrived[MB_ROWS : MB_ROWS + 1, 0:MB_ROWS]
+        squares = squares + arrived[MB_ROWS + 1 : MB_ROWS + 2, 0:MB_ROWS]
+        inverse = to_col(lax.rsqrt((squares_own[m, 0:1, 0:MB_ROWS] + squares) / D + 1e-05))
+        keyval = accum[m, :, lanes(Z + lax.div(z, per_kv))] + arrived[0:MB_ROWS]
+        keyval = keyval * inverse
         cos_kv = jnp.where(is_key, cos_ref[...], 1.0)
         sin_kv = jnp.where(is_key, sin_ref[...], 0.0)
         keyval = keyval * cos_kv + pltpu.roll(keyval, HD // 2, 1) * sin_kv
@@ -307,12 +313,12 @@
             recv_sems.at[s, m, 3],
             {"tensor": partner},
         )
-        return inverse
-
-    def attend(s, m, inverse, mask):
+        inverses[m] = jnp.broadcast_to(inverse, (MB_ROWS, HD))
+
+    def attend(s, m):
         drain(qrecv.at[s, m], recv_sems.at[s, m, 1])
         arrived = jnp.sum(qrecv[s, m].astype(F32), axis=0)
-        query = (accum[m, :, lanes(z)] + arrived) * inverse
+        query = (accum[m, :, lanes(z)] + arrived) * inverses[m]
         query = query * cos_ref[...] + pltpu.roll(query, HD // 2, 1) * sin_ref[...]
         drain(swrecv.at[s, m], recv_sems.at[s, m, 3])
         own, got = swsend[s, m], swrecv[s, m]
@@ -321,7 +327,7 @@
         scores = lax.dot_general(
             query.astype(BF16), keys, (((1,), (1,)), ((), ())), preferred_element_type=F32
         )
-        scores = jnp.where(mask, scores * scale, -jnp.inf)
+        scores = jnp.where(masks[m] > 0.5, scores * scale, -jnp.inf)
         highest = jnp.max(scores, axis=-1, keepdims=True)
         weights = jnp.exp(scores - highest)
         probs = (weights / jnp.sum(weights, axis=-1, keepdims=True)).astype(BF16)
@@ -336,50 +342,62 @@
                 {"tensor": tensor_peer(k)},
             )
 
-    def leave(s, m, last):
+    def leave(s, m):
         drain(att.at[s, m, :, pl.ds(0, (T - 1) * HD)], recv_sems.at[s, m, 4])
         projected = jnp.dot(att[s, m], wo[...], preferred_element_type=F32)
         xnew[s, m] = (xs[s, m, :, own_half].astype(F32) + projected).astype(BF16)
-        routes = [{"section": after}]
-        if not last:
-            routes.append({"section": after, "tensor": partner})
-        for route in routes:
+        def hop(target):
             push(
                 xnew.at[s, m],
                 xs.at[s + 1, m, :, own_half],
                 send_sems.at[s, m, 5],
                 recv_sems.at[s + 1, m, 5],
-                route,
+                {"section": after, "tensor": target},
             )
 
-    def step(s, first, last):
+        hop(t)
+
+        @pl.when(s < STEPS - 1)
+        def _():
+            hop(partner)
+
+    def each(phase):
+        def one(m, carry):
+            phase(m)
+            return carry
+
+        lax.fori_loop(0, MB_DEV, one, 0)
+
+    def step(s, carry):
         root = lax.rem(me - s + 2 * S, S)
-        each = range(MB_DEV)
-        if first:
-            gained = [project_kv(s, m, first) for m in each]
-            masks = [allowed_of(root, m) for m in each]
-            inverses = [swap(s, m) for m in each]
-            for m in each:
-                project_q(s, m, first, gained[m])
-        else:
-            for m in each:
-                project_q(s, m, first, project_kv(s, m, first))
-            masks = [allowed_of(root, m) for m in each]
-            inverses = [swap(s, m) for m in each]
-        for m in range(MB_DEV):
-            attend(s, m, inverses[m], masks[m])
-        for m in range(MB_DEV):
-            leave(s, m, last)
-
-    def middle(s, carry):
-        step(s, False, False)
+
+        def mask(m):
+            masks[m] = jnp.where(allowed_of(root, m), 1.0, 0.0)
+
+        def project(i, inner):
+            high, low = lax.div(i, MB_DEV), lax.rem(i, MB_DEV)
+            is_q = jnp.where(s == 0, high, low)
+            m = jnp.where(s == 0, low, high)
+
+            @pl.when(is_q == 0)
+            def _():
+                project_kv(s, m)
+
+            @pl.when(is_q == 1)
+            def _():
+                project_q(s, m)
+
+            return inner
+
+        lax.fori_loop(0, 2 * MB_DEV, project, 0)
+        each(mask)
+        each(lambda m: swap(s, m))
+        each(lambda m: attend(s, m))
+        each(lambda m: leave(s, m))
         return carry
 
     drain(gain_own, w_sems.at[1, 1])
-    step(0, True, False)
-    lax.fori_loop(1, STEPS - 1, middle, 0)
-    step(STEPS - 1, False, True)
-
+    lax.fori_loop(0, STEPS, step, 0)
     for m in range(MB_DEV):
         drain(xs.at[STEPS, m, :, pl.ds(0, width)], recv_sems.at[STEPS, m, 5])
         out[m * MB_ROWS : (m + 1) * MB_ROWS, :] = xs[STEPS, m, :, own_half]
@@ -392,7 +410,6 @@
 
     def finish(s, carry):
         for m in range(MB_DEV):
-            drain(ssrecv.at[s, m], send_sems.at[s, m, 0])
             drain(qsend.at[s, m], send_sems.at[s, m, 1])
             drain(kvsend.at[s, m], send_sems.at[s, m, 2])
             drain(swsend.at[s, m], send_sems.at[s, m, 3])
@@ -429,13 +446,15 @@
         pltpu.VMEM((MB_DEV, MB_ROWS, cols), F32),
         pltpu.VMEM(per + (Z - 1, MB_ROWS, HD), BF16),
         pltpu.VMEM(per + (Z - 1, MB_ROWS, HD), BF16),
-        pltpu.VMEM(per + (Z - 1, MB_ROWS, HD), BF16),
-        pltpu.VMEM(per + (Z - 1, MB_ROWS, HD), BF16),
-        pltpu.VMEM(per + (8, 2 * MB_ROWS), F32),
-        pltpu.VMEM(per + (Z - 1, 8, 2 * MB_ROWS), F32),
+        pltpu.VMEM(per + (Z - 1, MB_ROWS + SQ_ROWS, HD), BF16),
+        pltpu.VMEM(per + (Z - 1, MB_ROWS + SQ_ROWS, HD), BF16),
         pltpu.VMEM(per + (MB_ROWS, HD), BF16),
         pltpu.VMEM(per + (MB_ROWS, HD), BF16),
         pltpu.VMEM(per + (MB_ROWS, T * HD), BF16),
+        pltpu.VMEM((MB_DEV, MB_ROWS, 2 * width), BF16),
+        pltpu.VMEM((MB_DEV, 8, HD), F32),
+        pltpu.VMEM((MB_DEV, MB_ROWS, HD), F32),
+        pltpu.VMEM((MB_DEV, MB_ROWS, MB_ROWS), F32),
         pltpu.SemaphoreType.DMA((4 + KVH,)),
         pltpu.SemaphoreType.DMA((2, 5)),
         pltpu.SemaphoreType.DMA(per + (6,)),

time: 130 us -> 131 us (level)
  Pallas kernels: 128 us -> 130 us
    pallas_call x1, Pallas kernels: 128 us -> 130 us  [local(): pl.pallas_call(functools.partial(kernel, S, T), out_shape=jax.ShapeDtypeS...]
where the time goes in v6:
time: 131 us
  Pallas kernels  130 us (99%)
  local copies, waits for them, and re-layouts  1.67 us (1%)
    pallas_call x1, Pallas kernels, local(): pl.pallas_call(functools.partial(kernel, S, T), out_shape=jax.ShapeDtypeS...  130 us

profile of v6, /device:TPU:0, one launch (start us, length us, event | category | flops | bytes accessed | tf_op | source)
XLA Modules:
  0.0 131.2 jit_solution(12604923075486434035)
XLA Ops:
  0.0 129.6 %shard_map.100 = bf16[128,1024]{1,0:T(8,128)(2,1)} custom-call(bf16[64,1024]{1,0:T(8,128)(2,1)} %hidden.1, bf16[32,1024]{1,0:T(8,128)(2,1)} %audio.1, s32[1,128]{1,0:T(1,128)} %bitcast.1, s32[8,64]{1,0:T(8,128)} %segment.1, bf16[1,1024]{1,0:T(2,128)(2,1)} %gain.1, bf16[1,8192,128]{2,1,0:T(8,128)(2,1)} %wq.1, bf16[1,1024,1024]{2,1,0:T(8,128)(2,1)} %wkv.1, ...), custom_call_target="tpu_custom_call" | custom-call | flops 3221225472 | bytes 8388608 | tf_op jit(solution)/shard_map/pallas_call | solution.py:463
  129.6 1.7 %copy.12 = bf16[128,1024]{1,0:T(8,128)(2,1)} copy(bf16[128,1024]{1,0:T(8,128)(2,1)} %shard_map.100) | data formatting | bytes 524288

commit v7 on v6

--- a/solution.py
+++ b/solution.py
@@ -77,6 +77,7 @@
     squares_own,
     inverses,
     masks,
+    partial,
     local_sem,
     w_sems,
     send_sems,
@@ -125,7 +126,6 @@
         pltpu.make_async_copy(hidden, hid, local_sem.at[1]),
     ]
     late = [
-        pltpu.make_async_copy(wo_hbm.at[0], wo, local_sem.at[2]),
         pltpu.make_async_copy(
             wq.at[0, pair_rows(z), :], w_all.at[:, lanes(z)], local_sem.at[3]
         ),
@@ -136,6 +136,15 @@
                 wkv.at[0, :, lanes(2 * h + y)],
                 w_all.at[own_half, pl.ds(q_cols + h * HD, HD)],
                 local_sem.at[4 + h],
+            )
+        )
+
+    for head in range(T):
+        late.append(
+            pltpu.make_async_copy(
+                wo_hbm.at[0, pl.ds(head * HD, HD), :],
+                wo.at[pl.ds((head % 2 * Z + head // 2) * HD, HD), :],
+                local_sem.at[4 + KVH + head],
             )
         )
 
@@ -332,20 +341,39 @@
         weights = jnp.exp(scores - highest)
         probs = (weights / jnp.sum(weights, axis=-1, keepdims=True)).astype(BF16)
         attended = jnp.dot(probs, values, preferred_element_type=F32)
-        att[s, m, :, lanes(t)] = attended.astype(BF16)
-        for k in range(1, T):
+        att[s, m, :, lanes(y * Z + z)] = attended.astype(BF16)
+        for k in range(1, Z):
             push(
-                att.at[s, m, :, lanes(t)],
-                att.at[s, m, :, lanes(t)],
+                att.at[s, m, :, lanes(y * Z + z)],
+                att.at[s, m, :, lanes(y * Z + z)],
                 send_sems.at[s, m, 4],
                 recv_sems.at[s, m, 4],
-                {"tensor": tensor_peer(k)},
+                {"tensor": line_peer(k) * 2 + y},
             )
 
+    def parity(index):
+        return pl.ds(pl.multiple_of(index * q_cols, q_cols), q_cols)
+
+    def forward(s, m):
+        drain(att.at[s, m, :, pl.ds(0, (Z - 1) * HD)], recv_sems.at[s, m, 4])
+        push(
+            att.at[s, m, :, parity(y)],
+            att.at[s, m, :, parity(y)],
+            send_sems.at[s, m, 0],
+            recv_sems.at[s, m, 0],
+            {"tensor": partner},
+        )
+        projected = jnp.dot(
+            att[s, m, :, parity(y)], wo[parity(y), :], preferred_element_type=F32
+        )
+        partial[m] = xs[s, m, :, own_half].astype(F32) + projected
+
     def leave(s, m):
-        drain(att.at[s, m, :, pl.ds(0, (T - 1) * HD)], recv_sems.at[s, m, 4])
-        projected = jnp.dot(att[s, m], wo[...], preferred_element_type=F32)
-        xnew[s, m] = (xs[s, m, :, own_half].astype(F32) + projected).astype(BF16)
+        drain(att.at[s, m, :, pl.ds(0, q_cols)], recv_sems.at[s, m, 0])
+        projected = jnp.dot(
+            att[s, m, :, parity(1 - y)], wo[parity(1 - y), :], preferred_element_type=F32
+        )
+        xnew[s, m] = (partial[m] + projected).astype(BF16)
         def hop(target):
             push(
                 xnew.at[s, m],
@@ -393,6 +421,7 @@
         each(mask)
         each(lambda m: swap(s, m))
         each(lambda m: attend(s, m))
+        each(lambda m: forward(s, m))
         each(lambda m: leave(s, m))
         return carry
 
@@ -413,7 +442,8 @@
             drain(qsend.at[s, m], send_sems.at[s, m, 1])
             drain(kvsend.at[s, m], send_sems.at[s, m, 2])
             drain(swsend.at[s, m], send_sems.at[s, m, 3])
-            drain(att.at[s, m, :, pl.ds(0, (T - 1) * HD)], send_sems.at[s, m, 4])
+            drain(att.at[s, m, :, pl.ds(0, q_cols)], send_sems.at[s, m, 0])
+            drain(att.at[s, m, :, pl.ds(0, (Z - 1) * HD)], send_sems.at[s, m, 4])
             drain(xnew.at[s, m], send_sems.at[s, m, 5])
 
             @pl.when(s < STEPS - 1)
@@ -455,7 +485,8 @@
         pltpu.VMEM((MB_DEV, 8, HD), F32),
         pltpu.VMEM((MB_DEV, MB_ROWS, HD), F32),
         pltpu.VMEM((MB_DEV, MB_ROWS, MB_ROWS), F32),
-        pltpu.SemaphoreType.DMA((4 + KVH,)),
+        pltpu.VMEM((MB_DEV, MB_ROWS, width), F32),
+        pltpu.SemaphoreType.DMA((4 + KVH + T,)),
         pltpu.SemaphoreType.DMA((2, 5)),
         pltpu.SemaphoreType.DMA(per + (6,)),
         pltpu.SemaphoreType.DMA((STEPS + 1, MB_DEV, 6)),

time: 131 us -> 137 us (1.046)
  Pallas kernels: 130 us -> 135 us
    pallas_call x1, Pallas kernels: 130 us -> 135 us  [local(): pl.pallas_call(functools.partial(kernel, S, T), out_shape=jax.ShapeDtypeS...]
where the time goes in v7:
time: 137 us
  Pallas kernels  135 us (99%)
  local copies, waits for them, and re-layouts  1.67 us (1%)
    pallas_call x1, Pallas kernels, local(): pl.pallas_call(functools.partial(kernel, S, T), out_shape=jax.ShapeDtypeS...  135 us

profile of v7, /device:TPU:0, one launch (start us, length us, event | category | flops | bytes accessed | tf_op | source)
XLA Modules:
  0.0 136.7 jit_solution(1782278718463761657)
XLA Ops:
  0.0 135.0 %shard_map.100 = bf16[128,1024]{1,0:T(8,128)(2,1)} custom-call(bf16[64,1024]{1,0:T(8,128)(2,1)} %hidden.1, bf16[32,1024]{1,0:T(8,128)(2,1)} %audio.1, s32[1,128]{1,0:T(1,128)} %bitcast.1, s32[8,64]{1,0:T(8,128)} %segment.1, bf16[1,1024]{1,0:T(2,128)(2,1)} %gain.1, bf16[1,8192,128]{2,1,0:T(8,128)(2,1)} %wq.1, bf16[1,1024,1024]{2,1,0:T(8,128)(2,1)} %wkv.1, ...), custom_call_target="tpu_custom_call" | custom-call | flops 3221225472 | bytes 8388608 | tf_op jit(solution)/shard_map/pallas_call | solution.py:494
  135.0 1.7 %copy.12 = bf16[128,1024]{1,0:T(8,128)(2,1)} copy(bf16[128,1024]{1,0:T(8,128)(2,1)} %shard_map.100) | data formatting | bytes 524288

commit v8 on v6

v8 whole, which is shorter than its diff:
```python
import functools
import math

import jax
import jax.numpy as jnp
import numpy as np
from jax import lax
from jax.experimental import pallas as pl
from jax.experimental.pallas import tpu as pltpu
from jax.sharding import PartitionSpec as P

D = 8192
HD = 128
KVH = 4
MB_DEV = 2
AUD_MB = 32
TXT_MB = 32
AUD_DEV = 32
STEPS = 4
MB_ROWS = 64
SQ_ROWS = 16
ROWS = MB_DEV * MB_ROWS
HALVES = 2
MESH = pl.DeviceIdType.MESH
F32 = jnp.float32
BF16 = jnp.bfloat16


def rope_tables():
    position = np.arange(MB_ROWS, dtype=np.float32)
    freq = np.float32(500000.0) ** (-(2.0 * np.arange(HD // 2, dtype=np.float32)) / HD)
    angle = (position[:, None] * freq[None, :].astype(np.float32)).astype(np.float32)
    cosine, sine = np.cos(angle), np.sin(angle)
    return (
        np.tile(cosine, (MB_DEV, 2)).astype(np.float32),
        np.tile(np.concatenate([-sine, sine], 1), (MB_DEV, 1)).astype(np.float32),
    )


def iota(shape, dim):
    return lax.broadcasted_iota(jnp.int32, shape, dim)


def drain(ref, sem):
    pltpu.make_async_copy(ref, ref, sem).wait()


def kernel(
    S,
    T,
    hidden,
    audio,
    dest,
    segment,
    gain,
    wq,
    wkv,
    wo_hbm,
    cos_ref,
    sin_ref,
    out,
    w_all,
    wo,
    arecv,
    hid,
    gain_own,
    gain_pair,
    xs,
    xnew,
    accum,
    qsend,
    qrecv,
    kvsend,
    kvrecv,
    swsend,
    swrecv,
    att,
    xgain,
    squares_own,
    inverses,
    masks,
    local_sem,
    w_sems,
    send_sems,
    recv_sems,
):
    Z = T // 2
    width = gain.shape[1]
    cap = MB_DEV * AUD_MB // S
    shift = cap.bit_length() - 1
    per_kv = Z // KVH
    q_cols = Z * HD
    kv_cols = KVH * HD
    me = lax.axis_index("section")
    t = lax.axis_index("tensor")
    y = lax.rem(t, 2)
    z = lax.div(t, 2)
    partner = t + 1 - 2 * y
    after = lax.rem(me + 1, S)
    before = lax.rem(me + S - 1, S)
    own_half = pl.ds(pl.multiple_of(y * width, width), width)

    def lanes(index):
        return pl.ds(pl.multiple_of(index * HD, HD), HD)

    def pair_rows(index):
        return pl.ds(pl.multiple_of(index * 2 * width, 2 * width), 2 * width)

    def tensor_peer(k):
        return lax.rem(t + k, T)

    def line_peer(k):
        return lax.rem(z + k, Z)

    def push(src, dst, send, recv, device):
        pltpu.make_async_remote_copy(
            src_ref=src,
            dst_ref=dst,
            send_sem=send,
            recv_sem=recv,
            device_id=device,
            device_id_type=MESH,
        ).start()

    stage = [
        pltpu.make_async_copy(audio, arecv.at[me], local_sem.at[0]),
        pltpu.make_async_copy(hidden, hid, local_sem.at[1]),
    ]
    late = [
        pltpu.make_async_copy(wo_hbm.at[0], wo, local_sem.at[2]),
        pltpu.make_async_copy(
            wq.at[0, pair_rows(z), :], w_all.at[:, lanes(z)], local_sem.at[3]
        ),
    ]
    for h in range(KVH):
        late.append(
            pltpu.make_async_copy(
                wkv.at[0, :, lanes(2 * h + y)],
                w_all.at[own_half, pl.ds(q_cols + h * HD, HD)],
                local_sem.at[4 + h],
            )
        )

    barrier = pltpu.get_barrier_semaphore()

    def greet(device):
        pl.semaphore_signal(barrier, inc=1, device_id=device, device_id_type=MESH)

    for k in range(1, T):
        greet({"tensor": tensor_peer(k)})
    for k in range(1, S):
        greet({"section": lax.rem(me + k, S)})
    greet({"section": after, "tensor": partner})
    greet({"section": before, "tensor": partner})
    for copy in stage + late:
        copy.start()
    gain_own[...] = jnp.broadcast_to(gain[...].astype(F32), (8, width))
    gain_pair[:, own_half] = gain_own[...]
    pl.semaphore_wait(barrier, T + S)

    for k in range(1, S):
        push(
            audio,
            arecv.at[me],
            w_sems.at[0, 0],
            w_sems.at[1, 0],
            {"section": lax.rem(me + k, S)},
        )
    push(
        gain_own,
        gain_pair.at[:, own_half],
        w_sems.at[0, 1],
        w_sems.at[1, 1],
        {"tensor": partner},
    )
    for h in range(KVH):
        push(
            wkv.at[0, :, lanes(2 * h + 1 - y)],
            w_all.at[own_half, pl.ds(q_cols + h * HD, HD)],
            w_sems.at[0, 3],
            w_sems.at[1, 3],
            {"tensor": partner},
        )
    for k in range(1, Z):
        other = line_peer(k)
        push(
            wq.at[0, pair_rows(other), :],
            w_all.at[:, lanes(z)],
            w_sems.at[0, 4],
            w_sems.at[1, 4],
            {"tensor": other * 2 + y},
        )

    N = dest.shape[1]
    drow = dest[...].astype(F32)
    sub, lane = iota((N, N), 0), iota((N, N), 1)
    dcol = jnp.sum(jnp.where(sub == lane, drow, 0.0), axis=1, keepdims=True)
    same = (dcol == drow) & ((sub >> 5) == (lane >> 5)) & (sub < lane)
    rank = jnp.sum(jnp.where(same, 1.0, 0.0), axis=0, keepdims=True)
    block = (iota((1, N), 1) >> 5).astype(F32)
    slot = block * float(cap) + rank
    mine = drow == me.astype(F32)

    for copy in stage:
        copy.wait()
    drain(arecv.at[pl.ds(0, S - 1)], w_sems.at[1, 0])
    every_row = arecv[...].reshape(N, width)
    for m in range(MB_DEV):
        wanted = (iota((AUD_MB, N), 0) + m * AUD_MB).astype(F32)
        chosen = jnp.where((slot == wanted) & mine, 1.0, 0.0).astype(BF16)
        rows = jnp.dot(chosen, every_row, preferred_element_type=F32)
        top = m * MB_ROWS
        xs[0, top : top + AUD_MB, own_half] = rows.astype(BF16)
        text = hid[m * TXT_MB : (m + 1) * TXT_MB, :]
        xs[0, top + AUD_MB : top + MB_ROWS, own_half] = text
    push(
        xs.at[0, :, own_half],
        xs.at[0, :, own_half],
        w_sems.at[0, 2],
        recv_sems.at[0, 5],
        {"tensor": partner},
    )
    for copy in late:
        copy.wait()

    eye = iota((MB_ROWS, MB_ROWS), 0) == iota((MB_ROWS, MB_ROWS), 1)
    causal = iota((MB_ROWS, MB_ROWS), 1) <= iota((MB_ROWS, MB_ROWS), 0)
    scale = 1.0 / math.sqrt(HD)

    eye_all = iota((ROWS, ROWS), 0) == iota((ROWS, ROWS), 1)

    def to_col(row, where):
        return jnp.sum(jnp.where(where, row, 0.0), axis=1, keepdims=True)

    def to_row(col, where):
        return jnp.sum(jnp.where(where, col, 0.0), axis=0, keepdims=True)

    def allowed_of(root, m):
        seg_row = segment[pl.ds(root * MB_DEV + m, 1), :].astype(F32)
        seg_col = to_col(seg_row, eye)
        position = iota((MB_ROWS, N), 0)
        owner = ((position + m * AUD_MB) >> shift).astype(F32)
        named = (drow == root.astype(F32)) & (block == owner)
        count = jnp.sum(jnp.where(named, 1.0, 0.0), axis=1, keepdims=True)
        index = iota((MB_ROWS, 1), 0)
        within = (index & (cap - 1)).astype(F32)
        live = jnp.where((within < count) | (index >= AUD_MB), 1.0, 0.0)
        return causal & (seg_col == seg_row) & ((to_row(live, eye) > 0.5) | eye)

    def project_kv(s):
        @pl.when(s == 0)
        def _():
            drain(xs.at[0, :, pl.ds(0, width)], recv_sems.at[0, 5])

        @pl.when(s > 0)
        def _():
            drain(xs.at[s], recv_sems.at[s, 5])

        x = xs[s].astype(F32)
        sums = to_row(jnp.sum(x * x, axis=1, keepdims=True), eye_all)
        high = sums.astype(BF16).astype(F32)
        place = iota((SQ_ROWS, HD), 0)
        squares = jnp.where(place == 0, high, jnp.where(place == 1, sums - high, 0.0)).astype(BF16)
        squares_own[...] = jnp.broadcast_to(sums, (8, HD))
        xgain[...] = (x * gain_pair[0:1, :]).astype(BF16)

        @pl.when(s == 0)
        def _():
            drain(w_all.at[pl.ds(0, width), pl.ds(0, kv_cols)], w_sems.at[1, 3])
        accum[:, q_cols:] = jnp.dot(xgain[...], w_all[:, q_cols:], preferred_element_type=F32)
        for k in range(1, Z):
            other = line_peer(k)
            block_of = lanes(Z + lax.div(other, per_kv))
            kvsend[s, k - 1, 0:ROWS, :] = accum[:, block_of].astype(BF16)
            kvsend[s, k - 1, ROWS:, :] = squares
            push(
                kvsend.at[s, k - 1],
                kvrecv.at[s, k - 1],
                send_sems.at[s, 2],
                recv_sems.at[s, 2],
                {"tensor": other * 2 + y},
            )

    def project_q(s):
        @pl.when(s == 0)
        def _():
            drain(w_all.at[:, pl.ds(0, (Z - 1) * HD)], w_sems.at[1, 4])
        accum[:, :q_cols] = jnp.dot(xgain[...], w_all[:, :q_cols], preferred_element_type=F32)
        for k in range(1, Z):
            other = line_peer(k)
            qsend[s, k - 1] = accum[:, lanes(other)].astype(BF16)
            push(
                qsend.at[s, k - 1],
                qrecv.at[s, k - 1],
                send_sems.at[s, 1],
                recv_sems.at[s, 1],
                {"tensor": other * 2 + y},
            )

    is_key = y == 0

    def swap(s):
        drain(kvrecv.at[s], recv_sems.at[s, 2])
        arrived = jnp.sum(kvrecv[s].astype(F32), axis=0)
        squares = arrived[ROWS : ROWS + 1]
        squares = squares + arrived[ROWS + 1 : ROWS + 2]
        inverse = to_col(lax.rsqrt((squares_own[0:1, :] + squares) / D + 1e-05), eye_all)
        keyval = accum[:, lanes(Z + lax.div(z, per_kv))] + arrived[0:ROWS]
        keyval = keyval * inverse
        cos_kv = jnp.where(is_key, cos_ref[...], 1.0)
        sin_kv = jnp.where(is_key, sin_ref[...], 0.0)
        keyval = keyval * cos_kv + pltpu.roll(keyval, HD // 2, 1) * sin_kv
        swsend[s] = keyval.astype(BF16)
        push(
            swsend.at[s],
            swrecv.at[s],
            send_sems.at[s, 3],
            recv_sems.at[s, 3],
            {"tensor": partner},
        )
        inverses[...] = jnp.broadcast_to(inverse, (ROWS, HD))

    def attend(s):
        drain(qrecv.at[s], recv_sems.at[s, 1])
        arrived = jnp.sum(qrecv[s].astype(F32), axis=0)
        query = (accum[:, lanes(z)] + arrived) * inverses[...]
        query = query * cos_ref[...] + pltpu.roll(query, HD // 2, 1) * sin_ref[...]
        drain(swrecv.at[s], recv_sems.at[s, 3])
        own, got = swsend[s], swrecv[s]
        keys = jnp.where(is_key, own, got)
        values = jnp.where(is_key, got, own)
        query = query.astype(BF16)
        for m in range(MB_DEV):
            part = slice(m * MB_ROWS, (m + 1) * MB_ROWS)
            scores = lax.dot_general(
                query[part], keys[part], (((1,), (1,)), ((), ())), preferred_element_type=F32
            )
            scores = jnp.where(masks[m] > 0.5, scores * scale, -jnp.inf)
            highest = jnp.max(scores, axis=-1, keepdims=True)
            weights = jnp.exp(scores - highest)
            probs = (weights / jnp.sum(weights, axis=-1, keepdims=True)).astype(BF16)
            attended = jnp.dot(probs, values[part], preferred_element_type=F32)
            att[s, part, lanes(t)] = attended.astype(BF16)
        for k in range(1, T):
            push(
                att.at[s, :, lanes(t)],
                att.at[s, :, lanes(t)],
                send_sems.at[s, 4],
                recv_sems.at[s, 4],
                {"tensor": tensor_peer(k)},
            )

    def leave(s):
        drain(att.at[s, :, pl.ds(0, (T - 1) * HD)], recv_sems.at[s, 4])
        size = width // HALVES
        for half in range(HALVES):
            columns = slice(half * size, (half + 1) * size)
            place = pl.ds(pl.multiple_of(y * width + half * size, size), size)
            projected = jnp.dot(att[s], wo[:, columns], preferred_element_type=F32)
            xnew[s, :, columns] = (xs[s, :, place].astype(F32) + projected).astype(BF16)

            def hop(target):
                push(
                    xnew.at[s, :, columns],
                    xs.at[s + 1, :, place],
                    send_sems.at[s, 5],
                    recv_sems.at[s + 1, 5],
                    {"section": after, "tensor": target},
                )

            hop(t)

            @pl.when(s < STEPS - 1)
            def _():
                hop(partner)

    def step(s, carry):
        root = lax.rem(me - s + 2 * S, S)

        for m in range(MB_DEV):
            masks[m] = jnp.where(allowed_of(root, m), 1.0, 0.0)
        project_kv(s)

        @pl.when(s == 0)
        def _():
            swap(s)

        project_q(s)

        @pl.when(s > 0)
        def _():
            swap(s)

        attend(s)
        leave(s)
        return carry

    drain(gain_own, w_sems.at[1, 1])
    lax.fori_loop(0, STEPS, step, 0)
    drain(xs.at[STEPS, :, pl.ds(0, width)], recv_sems.at[STEPS, 5])
    out[...] = xs[STEPS, :, own_half]

    drain(arecv.at[pl.ds(0, S - 1)], w_sems.at[0, 0])
    drain(gain_own, w_sems.at[0, 1])
    drain(xs.at[0, :, pl.ds(0, width)], w_sems.at[0, 2])
    drain(w_all.at[pl.ds(0, width), pl.ds(0, kv_cols)], w_sems.at[0, 3])
    drain(w_all.at[:, pl.ds(0, (Z - 1) * HD)], w_sems.at[0, 4])

    def finish(s, carry):
        drain(qsend.at[s], send_sems.at[s, 1])
        drain(kvsend.at[s], send_sems.at[s, 2])
        drain(swsend.at[s], send_sems.at[s, 3])
        drain(att.at[s, :, pl.ds(0, (T - 1) * HD)], send_sems.at[s, 4])
        drain(xnew.at[s], send_sems.at[s, 5])

        @pl.when(s < STEPS - 1)
        def _():
            drain(xnew.at[s], send_sems.at[s, 5])

        return carry

    lax.fori_loop(0, STEPS, finish, 0)


def local(S, T, hidden, audio, audio_dest, segment, norm_gain, w_query, w_keyval, w_out):
    width = hidden.shape[1]
    rows = MB_DEV * MB_ROWS
    Z = T // 2
    cols = (Z + KVH) * HD
    cosine, sine = rope_tables()
    vmem = pl.BlockSpec(memory_space=pltpu.VMEM)
    hbm = pl.BlockSpec(memory_space=pl.ANY)
    scratch = [
        pltpu.VMEM((2 * width, cols), BF16),
        pltpu.VMEM(w_out.shape[1:], BF16),
        pltpu.VMEM((S, AUD_DEV, width), BF16),
        pltpu.VMEM((MB_DEV * TXT_MB, width), BF16),
        pltpu.VMEM((8, width), F32),
        pltpu.VMEM((8, 2 * width), F32),
        pltpu.VMEM((STEPS + 1, ROWS, 2 * width), BF16),
        pltpu.VMEM((STEPS, ROWS, width), BF16),
        pltpu.VMEM((ROWS, cols), F32),
        pltpu.VMEM((STEPS, Z - 1, ROWS, HD), BF16),
        pltpu.VMEM((STEPS, Z - 1, ROWS, HD), BF16),
        pltpu.VMEM((STEPS, Z - 1, ROWS + SQ_ROWS, HD), BF16),
        pltpu.VMEM((STEPS, Z - 1, ROWS + SQ_ROWS, HD), BF16),
        pltpu.VMEM((STEPS, ROWS, HD), BF16),
        pltpu.VMEM((STEPS, ROWS, HD), BF16),
        pltpu.VMEM((STEPS, ROWS, T * HD), BF16),
        pltpu.VMEM((ROWS, 2 * width), BF16),
        pltpu.VMEM((8, HD), F32),
        pltpu.VMEM((ROWS, HD), F32),
        pltpu.VMEM((MB_DEV, MB_ROWS, MB_ROWS), F32),
        pltpu.SemaphoreType.DMA((4 + KVH,)),
        pltpu.SemaphoreType.DMA((2, 5)),
        pltpu.SemaphoreType.DMA((STEPS, 6)),
        pltpu.SemaphoreType.DMA((STEPS + 1, 6)),
    ]
    return pl.pallas_call(
        functools.partial(kernel, S, T),
        out_shape=jax.ShapeDtypeStruct((rows, width), BF16),
        in_specs=[hbm, hbm, vmem, vmem, vmem, hbm, hbm, hbm, vmem, vmem],
        out_specs=vmem,
        scratch_shapes=scratch,
        compiler_params=pltpu.CompilerParams(
            collective_id=0, has_side_effects=True, vmem_limit_bytes=62 * 1024 * 1024
        ),
        cost_estimate=pl.CostEstimate(
            flops=STEPS * rows * width * (2 * cols + T * HD) * 2,
            bytes_accessed=8 * 1024 * 1024,
            transcendentals=0,
        ),
    )(
        hidden,
        audio,
        audio_dest.reshape(1, -1),
        segment,
        norm_gain,
        w_query,
        w_keyval,
        w_out,
        jnp.asarray(cosine),
        jnp.asarray(sine),
    )


def solution(mesh):
    in_specs = (
        P("section", "tensor"),
        P("section", "tensor"),
        P(),
        P(),
        P("section", "tensor"),
        P("section", None, "tensor"),
        P("section", "tensor", None),
        P("section", None, "tensor"),
    )
    out_specs = P("section", "tensor")
    body = functools.partial(local, mesh.shape["section"], mesh.shape["tensor"])
    return jax.shard_map(body, mesh=mesh, in_specs=in_specs, out_specs=out_specs, check_vma=False)
```

time: 131 us -> 142 us (1.084)
  Pallas kernels: 130 us -> 140 us
    pallas_call x1, Pallas kernels: 130 us -> 140 us  [local(): pl.pallas_call(functools.partial(kernel, S, T), out_shape=jax.ShapeDtypeS...]
where the time goes in v8:
time: 142 us; the launch traced here: 141 us
  Pallas kernels  140 us (99%)
  local copies, waits for them, and re-layouts  1.67 us (1%)
    pallas_call x1, Pallas kernels, local(): pl.pallas_call(functools.partial(kernel, S, T), out_shape=jax.ShapeDtypeS...  140 us

profile of v8, /device:TPU:0, one launch (start us, length us, event | category | flops | bytes accessed | tf_op | source)
XLA Modules:
  0.0 141.3 jit_solution(10282422046028969063)
XLA Ops:
  0.0 139.6 %shard_map.100 = bf16[128,1024]{1,0:T(8,128)(2,1)} custom-call(bf16[64,1024]{1,0:T(8,128)(2,1)} %hidden.1, bf16[32,1024]{1,0:T(8,128)(2,1)} %audio.1, s32[1,128]{1,0:T(1,128)} %bitcast.1, s32[8,64]{1,0:T(8,128)} %segment.1, bf16[1,1024]{1,0:T(2,128)(2,1)} %gain.1, bf16[1,8192,128]{2,1,0:T(8,128)(2,1)} %wq.1, bf16[1,1024,1024]{2,1,0:T(8,128)(2,1)} %wkv.1, ...), custom_call_target="tpu_custom_call" | custom-call | flops 3221225472 | bytes 8388608 | tf_op jit(solution)/shard_map/pallas_call | solution.py:459
  139.6 1.7 %copy.12 = bf16[128,1024]{1,0:T(8,128)(2,1)} copy(bf16[128,1024]{1,0:T(8,128)(2,1)} %shard_map.100) | data formatting | bytes 524288

commit v9 on v2

--- a/solution.py
+++ b/solution.py
@@ -18,6 +18,7 @@
 AUD_DEV = 32
 STEPS = 4
 MB_ROWS = 64
+HALVES = 2
 MESH = pl.DeviceIdType.MESH
 F32 = jnp.float32
 BF16 = jnp.bfloat16
@@ -338,33 +339,36 @@
 
     def leave(s, m, last):
         drain(att.at[s, m, :, pl.ds(0, (T - 1) * HD)], recv_sems.at[s, m, 4])
-        projected = jnp.dot(att[s, m], wo[...], preferred_element_type=F32)
-        xnew[s, m] = (xs[s, m, :, own_half].astype(F32) + projected).astype(BF16)
+        size = width // HALVES
         routes = [{"section": after}]
         if not last:
-            routes.append({"section": after, "tensor": partner})
-        for route in routes:
-            push(
-                xnew.at[s, m],
-                xs.at[s + 1, m, :, own_half],
-                send_sems.at[s, m, 5],
-                recv_sems.at[s + 1, m, 5],
-                route,
-            )
+            routes.insert(0, {"section": after, "tensor": partner})
+        for half in range(HALVES):
+            columns = slice(half * size, (half + 1) * size)
+            place = pl.ds(pl.multiple_of(y * width + half * size, size), size)
+            projected = jnp.dot(att[s, m], wo[:, columns], preferred_element_type=F32)
+            xnew[s, m, :, columns] = (xs[s, m, :, place].astype(F32) + projected).astype(BF16)
+            for route in routes:
+                push(
+                    xnew.at[s, m, :, columns],
+                    xs.at[s + 1, m, :, place],
+                    send_sems.at[s, m, 5],
+                    recv_sems.at[s + 1, m, 5],
+                    route,
+                )
 
     def step(s, first, last):
         root = lax.rem(me - s + 2 * S, S)
         each = range(MB_DEV)
+        masks = [allowed_of(root, m) for m in each]
         if first:
             gained = [project_kv(s, m, first) for m in each]
-            masks = [allowed_of(root, m) for m in each]
             inverses = [swap(s, m) for m in each]
             for m in each:
                 project_q(s, m, first, gained[m])
         else:
             for m in each:
                 project_q(s, m, first, project_kv(s, m, first))
-            masks = [allowed_of(root, m) for m in each]
             inverses = [swap(s, m) for m in each]
         for m in range(MB_DEV):
             attend(s, m, inverses[m], masks[m])

time: 130 us -> 129 us (level)
  no operation moved by 1% of the time
where the time goes in v9:
time: 129 us
  Pallas kernels  127 us (98%)
  local copies, waits for them, and re-layouts  1.67 us (1%)
    pallas_call x1, Pallas kernels, local(): pl.pallas_call(functools.partial(kernel, S, T), out_shape=jax.ShapeDtypeS...  127 us

profile of v9, /device:TPU:0, one launch (start us, length us, event | category | flops | bytes accessed | tf_op | source)
XLA Modules:
  0.0 129.0 jit_solution(11456095475740904562)
XLA Ops:
  0.0 127.3 %shard_map.100 = bf16[128,1024]{1,0:T(8,128)(2,1)} custom-call(bf16[64,1024]{1,0:T(8,128)(2,1)} %hidden.1, bf16[32,1024]{1,0:T(8,128)(2,1)} %audio.1, s32[1,128]{1,0:T(1,128)} %bitcast.1, s32[8,64]{1,0:T(8,128)} %segment.1, bf16[1,1024]{1,0:T(2,128)(2,1)} %gain.1, bf16[1,8192,128]{2,1,0:T(8,128)(2,1)} %wq.1, bf16[1,1024,1024]{2,1,0:T(8,128)(2,1)} %wkv.1, ...), custom_call_target="tpu_custom_call" | custom-call | flops 3221225472 | bytes 8388608 | tf_op jit(solution)/shard_map/pallas_call | solution.py:448
  127.3 1.7 %copy.12 = bf16[128,1024]{1,0:T(8,128)(2,1)} copy(bf16[128,1024]{1,0:T(8,128)(2,1)} %shard_map.100) | data formatting | bytes 524288

commit v10 on v9

--- a/solution.py
+++ b/solution.py
@@ -366,12 +366,15 @@
             inverses = [swap(s, m) for m in each]
             for m in each:
                 project_q(s, m, first, gained[m])
+            for m in each:
+                attend(s, m, inverses[m], masks[m])
         else:
             for m in each:
                 project_q(s, m, first, project_kv(s, m, first))
-            inverses = [swap(s, m) for m in each]
-        for m in range(MB_DEV):
-            attend(s, m, inverses[m], masks[m])
+                if m > 0:
+                    attend(s, m - 1, inverse, masks[m - 1])
+                inverse = swap(s, m)
+            attend(s, MB_DEV - 1, inverse, masks[-1])
         for m in range(MB_DEV):
             leave(s, m, last)
 

time: 129 us -> 131 us (1.016)
  Pallas kernels: 127 us -> 129 us
    pallas_call x1, Pallas kernels: 127 us -> 129 us  [local(): pl.pallas_call(functools.partial(kernel, S, T), out_shape=jax.ShapeDtypeS...]
where the time goes in v10:
time: 131 us; the launch traced here: 130 us
  Pallas kernels  129 us (98%)
  local copies, waits for them, and re-layouts  1.67 us (1%)
    pallas_call x1, Pallas kernels, local(): pl.pallas_call(functools.partial(kernel, S, T), out_shape=jax.ShapeDtypeS...  129 us

profile of v10, /device:TPU:0, one launch (start us, length us, event | category | flops | bytes accessed | tf_op | source)
XLA Modules:
  0.0 130.4 jit_solution(4178023625040221460)
XLA Ops:
  0.0 128.8 %shard_map.100 = bf16[128,1024]{1,0:T(8,128)(2,1)} custom-call(bf16[64,1024]{1,0:T(8,128)(2,1)} %hidden.1, bf16[32,1024]{1,0:T(8,128)(2,1)} %audio.1, s32[1,128]{1,0:T(1,128)} %bitcast.1, s32[8,64]{1,0:T(8,128)} %segment.1, bf16[1,1024]{1,0:T(2,128)(2,1)} %gain.1, bf16[1,8192,128]{2,1,0:T(8,128)(2,1)} %wq.1, bf16[1,1024,1024]{2,1,0:T(8,128)(2,1)} %wkv.1, ...), custom_call_target="tpu_custom_call" | custom-call | flops 3221225472 | bytes 8388608 | tf_op jit(solution)/shard_map/pallas_call | solution.py:451
  128.8 1.7 %copy.12 = bf16[128,1024]{1,0:T(8,128)(2,1)} copy(bf16[128,1024]{1,0:T(8,128)(2,1)} %shard_map.100) | data formatting | bytes 524288
